TPU v7x, 512 devices: a whole 4x8x8 slice. The times are simulated.
512 devices in a mesh: patch: 128 (over y, z, core), comp: 4 (over x).
Axes of the slice: x: 4, y: 8, z: 8, core: 2. Of those that a mesh axis runs over, the one named last changes fastest.
Arguments:
- vorticity: bfloat16 [128, 3, 32, 1024], P('patch', None, 'comp'), may hold values from -6 to 6
- pair_source: int32 [128, 3], P('patch'), may hold values from 0 to 127, as said below
- pair_offset: int32 [128, 3], P('patch'), may hold values from 0 to 26
- pair_count: int32 [128], P('patch'), may hold values from 1 to 3, as said below
- neighbours: int32 [128, 6], P('patch'), may hold values from -1 to 127, as said below
Outputs:
- velocity: float32 [128, 3, 32, 1024], P('patch', None, 'comp')
- stretching: float32 [128, 3, 32, 1024], P('patch', None, 'comp')
Inputs may be any that keep to these rules, and one draw needn't show every extreme that they name: pair_source[t, j] lies within 1 positions of t; the first pair_count[t] slots of a row name different patches, and slots from pair_count[t] on carry no pair. pair_count[t] is at most the number of patches within 1 positions of t, t included. `neighbours`: -1 marks the domain boundary; any other entry is a patch within 1 positions.
All inputs are finite; a program needn't handle non-finite values.
Results may differ from a plain program's by a relative error of at most 0.0035.
The roundings to bfloat16 on the way count: a program that leaves them out, or rounds other values in their place, can miss the bound.
Values may be sent and summed in bfloat16 or wider, within the bound.
A program may use at most 64 MiB of HBM per device.

v0:
```python
import jax
import jax.numpy as jnp
from jax import lax
from jax.sharding import PartitionSpec as P

CELL = 32
TERMS = 4
NEAR = 3


OPPOSITE = (1, 0, 3, 2, 5, 4)


def extended(shard, sides, width):
    for axis, dim in sides:
        devices, length = (lax.axis_size(axis), shard.shape[dim])
        up = [(i, (i + 1) % devices) for i in range(devices - 1)]
        down = [(j, i) for i, j in up]
        last = lax.slice_in_dim(shard, length - width, length, axis=dim)
        leading = lax.slice_in_dim(shard, 0, width, axis=dim)
        before = lax.ppermute(last, axis, up)
        after = lax.ppermute(leading, axis, down)
        shard = jnp.concatenate([before, shard, after], axis=dim)
    return shard


def term_weights():
    term_index = jnp.arange(TERMS, dtype=jnp.float32)
    widths = 1.5 * CELL / 4.0 ** (TERMS - 1 - term_index)
    return (widths, 0.08 / jnp.sqrt(widths))


def offset_tables(offset_code):
    widths, weights = term_weights()
    shifts = jnp.stack([offset_code // 9, offset_code // 3 % 3, offset_code % 3]) - 1
    cell_index = jnp.arange(CELL, dtype=jnp.int32)
    spacing = cell_index[None, :, None] - cell_index[None, None, :] - CELL * shifts[:, None, None]
    spacing = spacing.astype(jnp.float32)
    tables = jnp.exp(-spacing[None] ** 2 / (2.0 * widths[:, None, None, None] ** 2))
    return (tables.astype(jnp.bfloat16), weights)


def pair_field(source, offset_code):
    tables, weights = offset_tables(offset_code)
    along_z = jnp.einsum(
        "kab,ixyb->kixya", tables[:, 2], source, preferred_element_type=jnp.float32
    ).astype(jnp.bfloat16)
    along_y = jnp.einsum(
        "kab,kixbz->kixaz", tables[:, 1], along_z, preferred_element_type=jnp.float32
    ).astype(jnp.bfloat16)
    along_x = jnp.einsum(
        "kab,kibyz->kiayz", tables[:, 0], along_y, preferred_element_type=jnp.float32
    )
    return jnp.sum(weights[:, None, None, None, None] * along_x, axis=0)


def faces_of(values):
    return jnp.stack(
        [
            values[:, 0],
            values[:, -1],
            values[:, :, 0],
            values[:, :, -1],
            values[:, :, :, 0],
            values[:, :, :, -1],
        ]
    )


def ghosts_of(window_faces, neighbour_rows, window_start):
    flipped = jnp.array(OPPOSITE, dtype=jnp.int32)
    position = jnp.clip(neighbour_rows - window_start, 0, window_faces.shape[0] - 1)
    picked = window_faces[position, flipped]
    return jnp.where((neighbour_rows >= 0)[:, None, None, None], picked, 0.0)


def difference(values, ghosts, direction):
    lower_side = jnp.expand_dims(ghosts[2 * direction - 2], direction)
    higher = jnp.expand_dims(ghosts[2 * direction - 1], direction)
    padded = jnp.concatenate([lower_side, values, higher], axis=direction)
    length = values.shape[direction]
    return 0.5 * (
        lax.slice_in_dim(padded, 2, length + 2, axis=direction)
        - lax.slice_in_dim(padded, 0, length, axis=direction)
    )


def curl_of(values, ghosts):
    grad_x, grad_y, grad_z = [difference(values, ghosts, direction) for direction in (1, 2, 3)]
    return jnp.stack([grad_y[2] - grad_z[1], grad_z[0] - grad_x[2], grad_x[1] - grad_y[0]])


def stretch_slab(velocity, ghosts, vortex, slab_start):
    slab_cells = vortex.shape[1]
    grads = [
        lax.dynamic_slice_in_dim(difference(velocity, ghosts, direction), slab_start, slab_cells, 1)
        for direction in (1, 2, 3)
    ]
    return vortex[0] * grads[0] + vortex[1] * grads[1] + vortex[2] * grads[2]


def body(vorticity, pair_source, pair_offset, pair_count, neighbours):
    own_count = vorticity.shape[0]
    slab_cells = vorticity.shape[2]
    cube_shape = (CELL, CELL, CELL)
    planes = lax.all_gather(vorticity, "comp", axis=2, tiled=True)
    window = extended(planes, (("patch", 0),), own_count)
    window = window.reshape((window.shape[0], 3) + cube_shape)
    window_start = lax.axis_index("patch") * own_count - own_count
    member = lax.axis_index("comp")
    members = lax.axis_size("comp")
    slot_total = own_count * NEAR
    flat_source = pair_source.reshape(-1)
    flat_offset = pair_offset.reshape(-1)
    live_slot = (jnp.arange(NEAR, dtype=jnp.int32)[None, :] < pair_count[:, None]).reshape(-1)

    def add_slot(slot_id, active, running):
        patch_id = slot_id // NEAR
        position = jnp.clip(flat_source[slot_id] - window_start, 0, window.shape[0] - 1)
        source = lax.dynamic_index_in_dim(window, position, 0, keepdims=False)
        contribution = pair_field(source, flat_offset[slot_id])
        current = lax.dynamic_index_in_dim(running, patch_id, 0, keepdims=False)
        updated = current + jnp.where(active, contribution, 0.0)
        return lax.dynamic_update_index_in_dim(running, updated, patch_id, 0)

    zeros_init = jnp.zeros((own_count, 3) + cube_shape, jnp.float32)
    turn_count = (slot_total + members - 1) // members

    def slot_step(step_index, running):
        slot_id = member + members * step_index
        inside = slot_id < slot_total
        clipped = jnp.minimum(slot_id, slot_total - 1)
        return add_slot(clipped, inside & live_slot[clipped], running)

    partial_value = lax.fori_loop(0, turn_count, slot_step, zeros_init)
    vortex = vorticity.astype(jnp.float32).reshape(own_count, 3, slab_cells, CELL, CELL)
    out_shape = (own_count, 3, slab_cells, CELL * CELL)
    potential = lax.psum(partial_value, "comp")
    potential_faces = jax.vmap(faces_of)(potential)
    near_potential = extended(potential_faces, (("patch", 0),), own_count)
    potential_ghosts = jax.vmap(
        lambda neighbour_rows: ghosts_of(near_potential, neighbour_rows, window_start)
    )(neighbours)
    velocity = jax.vmap(curl_of)(potential, potential_ghosts)
    velocity_faces = jax.vmap(faces_of)(velocity)
    near_velocity = extended(velocity_faces, (("patch", 0),), own_count)
    velocity_ghosts = jax.vmap(
        lambda neighbour_rows: ghosts_of(near_velocity, neighbour_rows, window_start)
    )(neighbours)
    slab_start = member * slab_cells
    stretching = jax.vmap(
        lambda moving, borders, spinning: stretch_slab(moving, borders, spinning, slab_start)
    )(velocity, velocity_ghosts, vortex)
    velocity_slab = lax.dynamic_slice_in_dim(velocity, slab_start, slab_cells, 2)
    return (velocity_slab.reshape(out_shape), stretching.reshape(out_shape))


def solution(mesh):
    return jax.shard_map(
        body,
        mesh=mesh,
        in_specs=(
            P("patch", None, "comp", None),
            P("patch", None),
            P("patch", None),
            P("patch"),
            P("patch", None),
        ),
        out_specs=(P("patch", None, "comp", None), P("patch", None, "comp", None)),
        check_vma=False,
    )
```

profile of v0, /device:TPU:32, one launch (start us, length us, event | category | flops | bytes accessed | tf_op | source)
XLA Modules:
  0.0 204.3 jit_solution(13187805201549323778)
XLA Ops:
  7.2 12.7 %all_gather.3 = bf16[1,3,32,1024]{3,2,1,0:T(8,128)(2,1)S(1)} all-gather(bf16[1,3,8,1024]{3,2,1,0:T(8,128)(2,1)} %param.7), channel_id=1, replica_groups=mesh['patch'=128,'comp'=4] {'comp'}, dimensions={2}, use_global_device_ids=true | all-gather | bytes 245760 | tf_op jit(solution)/shard_map/all_gather | solution.py:106
  19.9 7.4 %collective-permute-start.1 = (bf16[1,3,32,1024]{3,2,1,0:T(8,128)(2,1)S(1)}, bf16[1,3,32,1024]{3,2,1,0:T(8,128)(2,1)S(1)}, u32[]{:S(2)}, u32[]{:S(2)}) collective-permute-start(bf16[1,3,32,1024]{3,2,1,0:T(8,128)(2,1)S(1)} %all_gather.3), channel_id=1, source_target_pairs={{4,0},{8,4},{12,8},{16,12},{20,16},{24,20},{28,24},{32,28},{36,32}... | collective-permute-start | bytes 589832 | tf_op jit(solution)/shard_map/ppermute | solution.py:22
  27.3 1.9 collective-permute-start
  29.3 1.4 fusion.33
  35.3 1.0 reshape.321
  37.6 0.7 constant_dynamic-slice_fusion.3
  39.8 0.7 fusion.18
  42.0 1.8 reshape.220
  43.8 1.7 convert_bitcast_fusion.1
  45.5 2.2 %convert_bitcast_fusion = bf16[4,3,32,32,32]{3,4,2,1,0:T(8,128)(2,1)S(1)} fusion(bf16[4,3,32,32,32]{4,3,0,2,1:T(8,128)(2,1)S(1)} %convert_bitcast_fusion.1, bf16[4,3,32,32]{3,2,0,1:T(8,128)(2,1)} %fusion.18), kind=kOutput, calls=%fused_computation.5 | convolution fusion | flops 25559040 | bytes 1605632 | tf_op jit(solution)/shard_map/while/body/eval_jaxpr/kab,kixbz->kixaz/dot_general | solution.py:48
  47.7 6.9 %copy.98 = bf16[4,3,32,32,32]{2,4,3,1,0:T(8,128)(2,1)} copy(bf16[4,3,32,32,32]{3,4,2,1,0:T(8,128)(2,1)S(1)} %convert_bitcast_fusion) | data formatting | bytes 1572864 | tf_op jit(solution)/shard_map/while/body/eval_jaxpr/convert_element_type | solution.py:50
  54.7 3.0 %multiply_reduce_fusion = f32[3,32,32,32]{3,2,1,0:T(8,128)S(1)} fusion(f32[4]{0:T(128)S(1)} %rsqrt_multiply_fusion, bf16[4,3,32,32,32]{2,4,3,1,0:T(8,128)(2,1)} %copy.98, bf16[4,3,32,32]{3,2,0,1:T(8,128)(2,1)} %fusion.18), kind=kOutput, calls=%fused_computation.2 | convolution fusion | flops 25853952 | bytes 3571728 | tf_op jit(solution)/shard_map/while/body/eval_jaxpr/kab,kibyz->kiayz/dot_general | solution.py:51
  57.7 1.3 select_bitcast_fusion
  59.7 0.7 fusion.31
  60.4 59.3 %all-reduce.2.cloned.1.call-done = f32[1,3,32,32,32]{2,4,3,1,0:T(8,128)} async-done(((f32[1,3,32,32,32]{2,4,3,1,0:T(8,128)}), f32[1,3,32,32,32]{2,4,3,1,0:T(8,128)}) %all-reduce.2.cloned.1.call-update) | async-done | bytes 393232 | tf_op jit(solution)/shard_map/psum | solution.py:138
  119.7 3.7 %fusion.30 = (f32[1,3,1,32,32]{2,4,3,1,0:T(8,128)S(1)}, f32[1,3,1,32,32]{2,4,3,1,0:T(8,128)}) fusion(f32[1,3,32,32,32]{2,4,3,1,0:T(8,128)} %all-reduce.2.cloned.1.call-done), kind=kLoop, calls=%fused_computation.96 | loop fusion | bytes 49152 | tf_op jit(solution)/shard_map/vmap()/slice | solution.py:61
  123.5 2.9 %copy.135 = f32[1,3,1,32,32]{3,4,1,2,0:T(8,128)} copy(f32[1,3,1,32,32]{2,4,3,1,0:T(8,128)} %get-tuple-element.80) | data formatting | bytes 24576 | tf_op jit(solution)/shard_map/vmap()/stack;vmap()/squeeze | solution.py:58
  126.4 1.5 bitcast_dynamic-update-slice_fusion.3
  127.8 1.5 copy.136
  129.3 1.4 bitcast_dynamic-update-slice_fusion.2
  133.3 5.1 %collective-permute-start.3 = (f32[1,6,3,32,32]{3,4,2,1,0:T(8,128)}, f32[1,6,3,32,32]{3,4,2,1,0:T(8,128)S(1)}, u32[]{:S(2)}, u32[]{:S(2)}) collective-permute-start(f32[1,6,3,32,32]{3,4,2,1,0:T(8,128)} %bitcast.152), channel_id=1, source_target_pairs={{4,0},{8,4},{12,8},{16,12},{20,16},{24,20},{28,24},{32,28},{36,32}... | collective-permute-start | bytes 221192 | tf_op jit(solution)/shard_map/ppermute | solution.py:22
  138.4 2.1 %collective-permute-start.2 = (f32[1,6,3,32,32]{3,4,2,1,0:T(8,128)}, f32[1,6,3,32,32]{3,4,2,1,0:T(8,128)S(1)}, u32[]{:S(2)}, u32[]{:S(2)}) collective-permute-start(f32[1,6,3,32,32]{3,4,2,1,0:T(8,128)} %bitcast.153), channel_id=1, source_target_pairs={{0,4},{4,8},{8,12},{12,16},{16,20},{20,24},{24,28},{28,32},{32,36}... | collective-permute-start | bytes 221192 | tf_op jit(solution)/shard_map/ppermute | solution.py:21
  140.6 0.7 slice.270
  141.3 0.7 mul.127
  142.0 0.7 mul.123
  142.7 0.7 mul.119
  143.4 6.6 %collective-permute-done.2 = f32[1,6,3,32,32]{3,4,2,1,0:T(8,128)S(1)} collective-permute-done((f32[1,6,3,32,32]{3,4,2,1,0:T(8,128)}, f32[1,6,3,32,32]{3,4,2,1,0:T(8,128)S(1)}, u32[]{:S(2)}, u32[]{:S(2)}) %collective-permute-start.2) | collective-permute-done | bytes 73760 | tf_op jit(solution)/shard_map/ppermute | solution.py:21
  150.0 1.0 pad_maximum_fusion.7
  151.8 1.4 copy.112
  153.2 2.4 %copy.111 = f32[1,3,1,32,32]{2,4,3,1,0:T(8,128)} copy(f32[1,3,1,32,32]{3,4,1,2,0:T(8,128)S(1)} %get-tuple-element.92) | data formatting | bytes 24576 | tf_op jit(solution)/shard_map/vmap()/broadcast_in_dim;vmap()/squeeze | solution.py:79
  155.5 3.3 %fusion.13 = (f32[1,3,32,32,32]{2,4,3,1,0:T(8,128)S(1)}, f32[1,3,32,32,32]{2,4,3,1,0:T(8,128)S(1)}, f32[1,3,32,32,32]{2,4,3,1,0:T(8,128)S(1)}) fusion(f32[1,3,32,32,32]{2,4,3,1,0:T(8,128)S(1)} %copy-done, f32[1,3,32,32,1]{2,4,3,1,0:T(1,128)S(1)} %bitcast.161, f32[1,3,32,32,1]{2,4,3,1,0:T(1,128)S(1)} %bitcast.160, ...), kind=kLoop, calls=%fused_computation.25 | loop fusion | flops 1179648 | bytes 1646592 | tf_op jit(solution)/shard_map/vmap()/mul | solution.py:82
  159.2 1.6 fusion.26
  160.8 1.7 fusion.28
  162.5 0.7 fusion.27
  163.2 2.2 %copy.147 = f32[1,3,1,32,32]{3,4,1,2,0:T(8,128)S(1)} copy(f32[1,3,1,32,32]{2,4,3,1,0:T(8,128)} %get-tuple-element.68) | data formatting | bytes 24576
  165.4 0.9 copy.148
  166.3 0.8 constant_dynamic-update-slice_fusion.3
  167.1 1.9 collective-permute-start.5
  169.0 2.6 %collective-permute-start.4 = (f32[1,6,3,32,32]{3,4,2,1,0:T(8,128)S(1)}, f32[1,6,3,32,32]{3,4,2,1,0:T(8,128)}, u32[]{:S(2)}, u32[]{:S(2)}) collective-permute-start(f32[1,6,3,32,32]{3,4,2,1,0:T(8,128)S(1)} %bitcast.156), channel_id=1, source_target_pairs={{0,4},{4,8},{8,12},{12,16},{16,20},{20,24},{24,28},{28,32},{32,36}... | collective-permute-start | bytes 221192 | tf_op jit(solution)/shard_map/ppermute | solution.py:21
  171.6 1.9 constant_dynamic-slice_fusion
  173.5 1.1 copy.140
  174.6 5.9 %collective-permute-done.4 = f32[1,6,3,32,32]{3,4,2,1,0:T(8,128)} collective-permute-done((f32[1,6,3,32,32]{3,4,2,1,0:T(8,128)S(1)}, f32[1,6,3,32,32]{3,4,2,1,0:T(8,128)}, u32[]{:S(2)}, u32[]{:S(2)}) %collective-permute-start.4) | collective-permute-done | bytes 73760 | tf_op jit(solution)/shard_map/ppermute | solution.py:21
  180.5 1.1 pad_maximum_fusion.8
  182.3 1.4 copy.121
  183.7 2.4 %copy.120 = f32[1,3,1,32,32]{2,4,3,1,0:T(8,128)} copy(f32[1,3,1,32,32]{3,4,1,2,0:T(8,128)S(1)} %get-tuple-element.84) | data formatting | bytes 24576 | tf_op jit(solution)/shard_map/vmap()/broadcast_in_dim;vmap()/squeeze | solution.py:79
  186.1 7.8 %fusion.9 = (f32[1,3,8,32,32]{2,4,3,1,0:T(8,128)}, f32[1,3,8,32,32]{2,4,3,1,0:T(8,128)}, f32[1,3,8,32,32]{2,4,3,1,0:T(8,128)}) fusion(s32[]{:T(128)} %bitcast.63, f32[1,3,32,32,32]{2,4,3,1,0:T(8,128)S(1)} %get-tuple-element.69, f32[1,3,1,32,32]{2,4,3,1,0:T(8,128)S(1)} %copy.121, f32[1,3,1,32,32]{2,4,3,1,0:T(8,128)} %copy.120, ...), kind=kLoop, calls=%fused_computation.17 | loop fusion | flops 294912 | bytes 761860 | tf_op jit(solution)/shard_map/vmap()/mul | solution.py:82
  193.9 2.0 copy.146
  196.8 0.7 multiply_add_fusion
  (58 shorter events, 7.6 us)
Async XLA Ops:
  7.2 112.6 %all-reduce.2.cloned.1.call-start = ((), (), s32[]{:S(2)}) async-start(), calls=%async_computation | async-start | bytes 3145728 | tf_op jit(solution)/shard_map/psum | solution.py:138
  19.9 22.0 %collective-permute-start.1 = (bf16[1,3,32,1024]{3,2,1,0:T(8,128)(2,1)S(1)}, bf16[1,3,32,1024]{3,2,1,0:T(8,128)(2,1)S(1)}, u32[]{:S(2)}, u32[]{:S(2)}) collective-permute-start(bf16[1,3,32,1024]{3,2,1,0:T(8,128)(2,1)S(1)} %all_gather.3), channel_id=1, source_target_pairs={{4,0},{8,4},{12,8},{16,12},{20,16},{24,20},{28,24},{32,28},{36,32}... | collective-permute-start | bytes 589832 | tf_op jit(solution)/shard_map/ppermute | solution.py:22
  27.3 14.6 %collective-permute-start = (bf16[1,3,32,1024]{3,2,1,0:T(8,128)(2,1)S(1)}, bf16[1,3,32,1024]{3,2,1,0:T(8,128)(2,1)S(1)}, u32[]{:S(2)}, u32[]{:S(2)}) collective-permute-start(bf16[1,3,32,1024]{3,2,1,0:T(8,128)(2,1)S(1)} %all_gather.3), channel_id=1, source_target_pairs={{0,4},{4,8},{8,12},{12,16},{16,20},{20,24},{24,28},{28,32},{32,36}... | collective-permute-start | bytes 589832 | tf_op jit(solution)/shard_map/ppermute | solution.py:21
  59.0 0.7 copy-start.9
  123.5 7.3 %copy-start = (f32[1,3,32,32,32]{2,4,3,1,0:T(8,128)S(1)}, f32[1,3,32,32,32]{2,4,3,1,0:T(8,128)}, u32[]{:S(2)}) copy-start(f32[1,3,32,32,32]{2,4,3,1,0:T(8,128)} %all-reduce.2.cloned.1.call-done) | copy-start | bytes 1179652
  126.4 14.9 %copy-start.5 = (f32[1,1,8,32,32]{4,3,2,1,0:T(8,128)S(1)}, f32[1,1,8,32,32]{4,3,2,1,0:T(8,128)}, u32[]{:S(2)}) copy-start(f32[1,1,8,32,32]{4,3,2,1,0:T(8,128)} %get-tuple-element.82) | copy-start | bytes 98308
  126.4 15.6 %copy-start.4 = (f32[1,1,8,32,32]{4,3,2,1,0:T(8,128)S(1)}, f32[1,1,8,32,32]{4,3,2,1,0:T(8,128)}, u32[]{:S(2)}) copy-start(f32[1,1,8,32,32]{4,3,2,1,0:T(8,128)} %get-tuple-element.83) | copy-start | bytes 98308
  126.4 16.3 %copy-start.3 = (f32[1,1,8,32,32]{4,3,2,1,0:T(8,128)S(1)}, f32[1,1,8,32,32]{4,3,2,1,0:T(8,128)}, u32[]{:S(2)}) copy-start(f32[1,1,8,32,32]{4,3,2,1,0:T(8,128)} %get-tuple-element.81) | copy-start | bytes 98308
  133.3 10.1 %collective-permute-start.3 = (f32[1,6,3,32,32]{3,4,2,1,0:T(8,128)}, f32[1,6,3,32,32]{3,4,2,1,0:T(8,128)S(1)}, u32[]{:S(2)}, u32[]{:S(2)}) collective-permute-start(f32[1,6,3,32,32]{3,4,2,1,0:T(8,128)} %bitcast.152), channel_id=1, source_target_pairs={{4,0},{8,4},{12,8},{16,12},{20,16},{24,20},{28,24},{32,28},{36,32}... | collective-permute-start | bytes 221192 | tf_op jit(solution)/shard_map/ppermute | solution.py:22
  138.4 11.6 %collective-permute-start.2 = (f32[1,6,3,32,32]{3,4,2,1,0:T(8,128)}, f32[1,6,3,32,32]{3,4,2,1,0:T(8,128)S(1)}, u32[]{:S(2)}, u32[]{:S(2)}) collective-permute-start(f32[1,6,3,32,32]{3,4,2,1,0:T(8,128)} %bitcast.153), channel_id=1, source_target_pairs={{0,4},{4,8},{8,12},{12,16},{16,20},{20,24},{24,28},{28,32},{32,36}... | collective-permute-start | bytes 221192 | tf_op jit(solution)/shard_map/ppermute | solution.py:21
  167.1 7.5 %collective-permute-start.5 = (f32[1,6,3,32,32]{3,4,2,1,0:T(8,128)S(1)}, f32[1,6,3,32,32]{3,4,2,1,0:T(8,128)}, u32[]{:S(2)}, u32[]{:S(2)}) collective-permute-start(f32[1,6,3,32,32]{3,4,2,1,0:T(8,128)S(1)} %bitcast.155), channel_id=1, source_target_pairs={{4,0},{8,4},{12,8},{16,12},{20,16},{24,20},{28,24},{32,28},{36,32}... | collective-permute-start | bytes 221192 | tf_op jit(solution)/shard_map/ppermute | solution.py:22
  169.0 11.5 %collective-permute-start.4 = (f32[1,6,3,32,32]{3,4,2,1,0:T(8,128)S(1)}, f32[1,6,3,32,32]{3,4,2,1,0:T(8,128)}, u32[]{:S(2)}, u32[]{:S(2)}) collective-permute-start(f32[1,6,3,32,32]{3,4,2,1,0:T(8,128)S(1)} %bitcast.156), channel_id=1, source_target_pairs={{0,4},{4,8},{8,12},{12,16},{16,20},{20,24},{24,28},{28,32},{32,36}... | collective-permute-start | bytes 221192 | tf_op jit(solution)/shard_map/ppermute | solution.py:21
  193.9 2.0 copy-start.2
  193.9 2.4 %copy-start.1 = (f32[1,3,8,32,32]{2,4,3,1,0:T(8,128)S(1)}, f32[1,3,8,32,32]{2,4,3,1,0:T(8,128)}, u32[]{:S(2)}) copy-start(f32[1,3,8,32,32]{2,4,3,1,0:T(8,128)} %get-tuple-element.62) | copy-start | bytes 294916
  195.9 0.9 copy-start.6
  195.9 0.9 copy-start.7
  195.9 0.9 copy-start.8
Sparse Core Ops, SparseCore 0:
  59.2 60.5 all-reduce.1
where the time goes:
time: 205 us; the launch traced here: 204 us
  waiting for transfers between devices  71.8 us (35%)
  local copies, waits for them, and re-layouts  49 us (24%)
  between operations  21.6 us (11%)
  starting transfers between devices  21.2 us (10%)
  other arithmetic  21.2 us (10%)
  blocking collectives  12.7 us (6%)
  matrix products  6.96 us (3%)
    psum x1, waiting for transfers between devices, body(): potential = lax.psum(partial_value, 'comp')  59.3 us
    ppermute x3, starting transfers between devices, extended(): after = lax.ppermute(leading, axis, down)  14.5 us
    all_gather x1, blocking collectives, body(): planes = lax.all_gather(vorticity, 'comp', axis=2, tiled=True)  12.7 us
    ppermute x3, waiting for transfers between devices, extended(): before = lax.ppermute(last, axis, up)  12.4 us
    mul x2, other arithmetic, difference(): 0.5 * (lax.slice_in_dim(padded, 2, length + 2, axis=direction) - lax.slic...  11.1 us
    unnamed x32, local copies, waits for them, and re-layouts  9.3 us
    convert_element_type x1, local copies, waits for them, and re-layouts, pair_field(): along_y = jnp.einsum('kab,kixbz->kixaz', tables[:, 1], along_z, preferred...  6.94 us
    ppermute x3, starting transfers between devices, extended(): before = lax.ppermute(last, axis, up)  6.65 us
  transfers between devices with their start and end apart: 7, of which 3 were waited for; matrix products, arithmetic and copies ran while one was open for 6% of the time, Pallas kernels for 0%

commit v1 on v0

v1 whole, which is shorter than its diff:
```python
import functools

import jax
import jax.numpy as jnp
from jax import lax
from jax.experimental import pallas as pl
from jax.experimental.pallas import tpu as pltpu
from jax.sharding import PartitionSpec as P

CELL = 32
TERMS = 4
NEAR = 3
MEMBERS = 4
SLAB = CELL // MEMBERS
COMPONENTS = 3
CHUNK = 4 * COMPONENTS * SLAB
PATCH_ROWS = MEMBERS * CHUNK
TILE = 256
HALO = 16
W0 = 0.08 / 0.75 ** 0.5
F32 = jnp.float32
BF16 = jnp.bfloat16
MESH_ID = pl.DeviceIdType.MESH


def iota(shape, dim):
    return lax.broadcasted_iota(jnp.int32, shape, dim)


def lane_roll(values, shift):
    shift = shift % 128
    return values if shift == 0 else pltpu.roll(values, shift, values.ndim - 1)


def row_roll(values, shift):
    shift = shift % 8
    if shift == 0:
        return values
    grouped = values.reshape(-1, 8, 128)
    return pltpu.roll(grouped, shift, 1).reshape(values.shape)


def slot_of(position, src_ref, off_ref, cnt_ref, patch):
    code = jnp.int32(13)
    live = jnp.int32(0)
    count = cnt_ref[0]
    for j in range(NEAR):
        hit = (count > j) & (src_ref[0, j] == patch - 1 + position)
        code = jnp.where(hit, off_ref[0, j], code)
        live = jnp.where(hit, 1, live)
    shifts = (lax.div(code, 9) - 1, lax.rem(lax.div(code, 3), 3) - 1, lax.rem(code, 3) - 1)
    return shifts, live


def gauss(spacing, scale):
    spacing = spacing.astype(F32)
    return jnp.exp(-(spacing * spacing / 1.125) * scale)


def write_tables(position, shifts, live, member, wz_ref, wy_ref, lx_ref):
    shift_x, shift_y, shift_z = shifts
    rows = iota((CELL, TILE), 0)
    cols = iota((CELL, TILE), 1)
    gap_z = (cols >> 3) - rows - CELL * shift_z
    gap_y = ((cols >> 5) + 8 * ((cols >> 3) & 3)) - rows - CELL * shift_y
    low = cols & 7
    low8 = iota((8, TILE), 1) & 7
    for k in range(TERMS):
        scale = 1.0 / 16.0 ** k
        table = gauss(gap_z, scale)
        wz_ref[position * TERMS + k] = jnp.concatenate(
            [jnp.where(low == y, table, 0.0) for y in range(8)], axis=0
        ).astype(BF16)
        table = gauss(gap_y, scale)
        wy_ref[position * TERMS + k] = jnp.concatenate(
            [jnp.where(low8 == z, table[8 * h : 8 * h + 8], 0.0) for h in range(4) for z in range(8)],
            axis=0,
        ).astype(BF16)
    row = iota((HALO, 128), 0)
    col = iota((HALO, 128), 1)
    plane = (SLAB * member + jnp.where(row < 12, row, row - HALO)) & (CELL - 1)
    term = col >> 5
    scale = jnp.where(term == 0, 1.0, jnp.where(term == 1, 1 / 16, jnp.where(term == 2, 1 / 256, 1 / 4096)))
    weight = jnp.where(term == 0, 1.0, jnp.where(term == 1, 0.5, jnp.where(term == 2, 0.25, 0.125)))
    table = gauss(plane - (col & (CELL - 1)) - CELL * shift_x, scale).astype(BF16).astype(F32)
    lx_ref[position] = (table * weight * live.astype(F32)).astype(BF16)


def pair_products(position, gbuf, wz_ref, wy_ref, lx_ref, rbuf, acc, first):
    lower = iota((MEMBERS, 24, 128), 2) < 64
    for k in range(TERMS):
        along_z = jnp.dot(gbuf[position], wz_ref[position * TERMS + k], preferred_element_type=F32)
        along_z = along_z.reshape(MEMBERS, 4, 24, TILE)
        blocks = [[None] * 2 for _ in range(4)]
        for pair in range(2):
            for half in range(2):
                a = along_z[:, 2 * pair, :, 128 * half : 128 * half + 128]
                b = along_z[:, 2 * pair + 1, :, 128 * half : 128 * half + 128]
                blocks[2 * half][pair] = jnp.where(lower, a, lane_roll(b, 64))
                blocks[2 * half + 1][pair] = jnp.where(lower, lane_roll(a, 64), b)
        pieces = []
        for block in blocks:
            joined = jnp.concatenate(block, axis=2)
            for i in range(COMPONENTS):
                pieces.append(joined[:, 8 * i : 8 * i + 8].reshape(CELL, TILE))
        swapped = jnp.concatenate(pieces, axis=0).astype(BF16)
        along_y = jnp.dot(swapped, wy_ref[position * TERMS + k], preferred_element_type=F32).astype(BF16)
        rbuf[:, CELL * k : CELL * k + CELL, :] = along_y.reshape(12, CELL, TILE)
    for block in range(12):
        term = jnp.dot(lx_ref[position], rbuf[block], preferred_element_type=F32)
        acc[block] = term if first else acc[block] + term


def potential_of(acc):
    lane = iota((2 * HALO, 128), 1)
    bit4 = (lane & 16) == 0
    bit3 = (lane & 8) == 0
    out = []
    for i in range(COMPONENTS):
        a = []
        for block in range(4):
            tile = acc[3 * block + i] * W0
            a.append(jnp.concatenate([tile[:, :128], tile[:, 128:]], axis=0))
        b = [
            jnp.where(bit4, a[0], lane_roll(a[2], 16)),
            jnp.where(bit4, a[1], lane_roll(a[3], 16)),
            jnp.where(bit4, lane_roll(a[0], -16), a[2]),
            jnp.where(bit4, lane_roll(a[1], -16), a[3]),
        ]
        d = [
            jnp.where(bit3, b[0], lane_roll(b[1], 8)),
            jnp.where(bit3, lane_roll(b[0], -8), b[1]),
            jnp.where(bit3, b[2], lane_roll(b[3], 8)),
            jnp.where(bit3, lane_roll(b[2], -8), b[3]),
        ]
        out.append(jnp.concatenate(d, axis=0))
    return out


def z_slots(count):
    for j in range(count):
        for v in range(8):
            yield j, v, v % 2, 2 * (count * (v // 2) + j) + 1


def pack_z(fields, rows):
    shape = (rows, 128)
    lane = iota(shape, 1) & 31
    packed = [jnp.zeros(shape, F32)] * 2
    for j, v, u, s in z_slots(len(fields)):
        mine = (lane == s) | (lane == s - 1)
        packed[u] = jnp.where(mine, lane_roll(fields[j][rows * v : rows * v + rows], s), packed[u])
    return packed


def unpack_z(packed, count, rows):
    above = [[None] * 8 for _ in range(count)]
    below = [[None] * 8 for _ in range(count)]
    for j, v, u, s in z_slots(count):
        above[j][v] = lane_roll(packed[u], 31 - s)
        below[j][v] = lane_roll(packed[u], 97 - s)
    return (
        [jnp.concatenate(x, axis=0) for x in above],
        [jnp.concatenate(x, axis=0) for x in below],
    )


def grad_z(field, above, below):
    z = iota(field.shape, 1) & 31
    higher = jnp.where(z == 31, above, lane_roll(field, -1))
    lower = jnp.where(z == 0, below, lane_roll(field, 1))
    return 0.5 * (higher - lower)


def pack_y(field, rows):
    lower = iota((rows, 128), 1) < 64
    return jnp.where(lower, field[:rows], field[7 * rows :])


def grad_y(field, ghost, rows):
    lane = iota(field.shape, 1)
    moved = lane_roll(field, -32)
    following = jnp.concatenate([moved[rows:], lane_roll(ghost, -32)], axis=0)
    higher = jnp.where(lane < 96, moved, following)
    moved = lane_roll(field, 32)
    previous = jnp.concatenate([lane_roll(ghost, 32), moved[:-rows]], axis=0)
    lower = jnp.where(lane >= 32, moved, previous)
    return 0.5 * (higher - lower)


def halves(field):
    grouped = field.reshape(8, 2, 8, 128)
    return grouped[:, 0], grouped[:, 1]


def pack_x(fields, member):
    groups = []
    for field in fields:
        low, high = halves(field)
        at_end = jnp.full(low.shape, member, jnp.int32) == MEMBERS - 1
        first = jnp.where(at_end, high, low)
        last = jnp.where(at_end, low, high)
        row = iota((2, 8, 128), 1)
        packed = jnp.zeros((2, 8, 128), F32)
        for s in range(4):
            a = pltpu.roll(first[2 * s : 2 * s + 2], 7 - s, 1)
            b = pltpu.roll(last[2 * s : 2 * s + 2], s + 1, 1)
            packed = jnp.where(row == 7 - s, a, jnp.where(row == s, b, packed))
        groups.append(packed)
    return groups


def unpack_x(packed):
    above = jnp.concatenate([packed if s == 0 else pltpu.roll(packed, s, 1) for s in range(4)], axis=0)
    below = jnp.concatenate([packed if s == 0 else pltpu.roll(packed, 8 - s, 1) for s in range(4)], axis=0)
    return above, below


def grad_x(field, packed, member, own_only):
    low, high = halves(field)
    above, below = unpack_x(packed)
    row = iota(low.shape, 1)
    device = jnp.full(low.shape, member, jnp.int32)
    first = device == 0
    last = device == MEMBERS - 1
    moved_low = pltpu.roll(low, 7, 1)
    moved_high = pltpu.roll(high, 7, 1)
    up_low = jnp.where(row == 7, jnp.where(last, above, moved_high), moved_low)
    back_low = pltpu.roll(low, 1, 1)
    back_high = pltpu.roll(high, 1, 1)
    down_low = jnp.where(row == 0, jnp.where(first, below, back_high), back_low)
    own = 0.5 * (up_low - down_low)
    if own_only:
        return own.reshape(64, 128)
    up_high = jnp.where(row == 7, jnp.where(first, above, moved_low), moved_high)
    down_high = jnp.where(row == 0, jnp.where(last, below, back_low), back_high)
    other = 0.5 * (up_high - down_high)
    return jnp.stack([own, other], axis=1).reshape(128, 128)


def own_rows(field):
    return halves(field)[0].reshape(64, 128)


def kernel(patches, src_ref, off_ref, cnt_ref, nb_ref, vort_ref, vel_ref, str_ref,
           gbuf, wz_ref, wy_ref, lx_ref, rbuf, acc, pbuf, vbuf,
           xsend, fsend, grecv, psend, precv, vsend, vrecv):
    patch = lax.axis_index("patch")
    member = lax.axis_index("comp")
    left = lax.rem(patch + patches - 1, patches)
    right = lax.rem(patch + 1, patches)

    def chunk(position, owner):
        return gbuf.at[position, pl.ds(pl.multiple_of(owner * CHUNK, CHUNK), CHUNK)]

    def other(step):
        return lax.rem(member + step, MEMBERS)

    barrier = pltpu.get_barrier_semaphore()
    partners = [(patch, other(d)) for d in (1, 2, 3)] + [(left, member), (right, member)]
    for partner in partners:
        pl.semaphore_signal(barrier, inc=1, device_id=partner, device_id_type=MESH_ID)

    cells = [vort_ref[0, i].astype(F32) for i in range(COMPONENTS)]
    staged = jnp.concatenate(
        [cells[i][:, TILE * q : TILE * q + TILE] for q in range(4) for i in range(COMPONENTS)], axis=0
    ).astype(BF16)
    gbuf[1, pl.ds(pl.multiple_of(member * CHUNK, CHUNK), CHUNK), :] = staged
    pl.semaphore_wait(barrier, len(partners))

    def across(step):
        return pltpu.make_async_remote_copy(
            src_ref=chunk(1, member), dst_ref=chunk(1, member),
            send_sem=xsend.at[step - 1], recv_sem=grecv.at[MEMBERS + member],
            device_id=(patch, other(step)), device_id_type=MESH_ID,
        )

    def onward(owner, step):
        target, place = ((right, 0), (left, 2))[step]
        return pltpu.make_async_remote_copy(
            src_ref=chunk(1, owner), dst_ref=chunk(place, owner),
            send_sem=fsend.at[2 * owner + step], recv_sem=grecv.at[place * MEMBERS + owner],
            device_id=(target, member), device_id_type=MESH_ID,
        )

    def arrived(position, owner):
        pltpu.make_async_remote_copy(
            src_ref=chunk(position, owner), dst_ref=chunk(position, owner),
            send_sem=xsend.at[0], recv_sem=grecv.at[position * MEMBERS + owner],
            device_id=(right, member), device_id_type=MESH_ID,
        ).wait_recv()

    across(1).start()
    across(3).start()
    onward(member, 0).start()
    onward(member, 1).start()
    across(2).start()

    def tables(position):
        shifts, live = slot_of(position, src_ref, off_ref, cnt_ref, patch)
        write_tables(position, shifts, live, member, wz_ref, wy_ref, lx_ref)

    def products(position, first):
        pair_products(position, gbuf, wz_ref, wy_ref, lx_ref, rbuf, acc, first)

    tables(1)
    for step in (1, 3, 2):
        owner = other(step)
        arrived(1, owner)
        onward(owner, 0).start()
        onward(owner, 1).start()
    tables(0)
    tables(2)
    products(1, True)
    for position in (0, 2):
        for step in (0, 1, 3, 2):
            arrived(position, other(step))
        products(position, False)

    def exchange(buffer, send, recv):
        copies = []
        for step, (target, place) in enumerate(((right, 0), (left, 2))):
            copies.append(pltpu.make_async_remote_copy(
                src_ref=buffer.at[1], dst_ref=buffer.at[place],
                send_sem=send.at[step], recv_sem=recv.at[step],
                device_id=(target, member), device_id_type=MESH_ID,
            ))
        for copy in copies:
            copy.start()
        return copies

    def pick(buffer, face, index, shape):
        source = jnp.full(shape, nb_ref[0, face], jnp.int32)
        parts = [buffer[place, index].reshape(shape) for place in range(3)]
        chosen = jnp.where(source < patch, parts[0], jnp.where(source == patch, parts[1], parts[2]))
        return jnp.where(source < 0, 0.0, chosen)

    def ghosts(buffer, rows, z_count, y_count, x_count):
        shape = (rows, 128)
        groups = rows // 8
        lane = iota(shape, 1)
        zs, ys, xs = [], [], []
        for u in range(2):
            index = pl.ds(u * groups, groups)
            zs.append(jnp.where((lane & 1) == 1, pick(buffer, 5, index, shape), pick(buffer, 4, index, shape)))
        at = 2 * groups
        for j in range(y_count):
            index = pl.ds(at, groups)
            ys.append(jnp.where(lane < 64, pick(buffer, 3, index, shape), pick(buffer, 2, index, shape)))
            at += groups
        shape = (2, 8, 128)
        row = iota(shape, 1)
        for j in range(x_count):
            index = pl.ds(at, 2)
            xs.append(jnp.where(row < 4, pick(buffer, 0, index, shape), pick(buffer, 1, index, shape)))
            at += 2
        return zs, ys, xs

    px, py, pz = potential_of(acc)
    packs = pack_z([px, py], HALO) + [pack_y(px, HALO), pack_y(pz, HALO)]
    for index, part in enumerate(packs):
        pbuf[1, 2 * index : 2 * index + 2] = part.reshape(2, 8, 128)
    for index, part in enumerate(pack_x([py, pz], member)):
        pbuf[1, 8 + 2 * index : 10 + 2 * index] = part
    copies = exchange(pbuf, psend, precv)
    for copy in copies:
        copy.wait_recv()
    zs, ys, xs = ghosts(pbuf, HALO, 2, 2, 2)
    above, below = unpack_z(zs, 2, HALO)
    vx = grad_y(pz, ys[1], HALO) - grad_z(py, above[1], below[1])
    vy = grad_z(px, above[0], below[0]) - grad_x(pz, xs[1], member, False)
    vz = grad_x(py, xs[0], member, False) - grad_y(px, ys[0], HALO)
    velocity = [vx, vy, vz]
    own = [own_rows(v) for v in velocity]
    packs = pack_z(own, 8) + [pack_y(v, 8) for v in own]
    for index, part in enumerate(packs):
        vbuf[1, index] = part
    for index, part in enumerate(pack_x(velocity, member)):
        vbuf[1, 5 + 2 * index : 7 + 2 * index] = part
    vcopies = exchange(vbuf, vsend, vrecv)
    for i in range(COMPONENTS):
        for v in range(8):
            vel_ref[0, i, :, 128 * v : 128 * v + 128] = own[i][8 * v : 8 * v + 8]
    for copy in vcopies:
        copy.wait_recv()
    zs, ys, xs = ghosts(vbuf, 8, 3, 3, 3)
    above, below = unpack_z(zs, 3, 8)
    spin = [
        jnp.concatenate([vort_ref[0, i, :, 128 * v : 128 * v + 128].astype(F32) for v in range(8)], axis=0)
        for i in range(COMPONENTS)
    ]
    for i in range(COMPONENTS):
        total = (
            spin[0] * grad_x(velocity[i], xs[i], member, True)
            + spin[1] * grad_y(own[i], ys[i], 8)
            + spin[2] * grad_z(own[i], above[i], below[i])
        )
        for v in range(8):
            str_ref[0, i, :, 128 * v : 128 * v + 128] = total[8 * v : 8 * v + 8]

    for step in (1, 2, 3):
        across(step).wait_send()
    for owner in range(MEMBERS):
        onward(owner, 0).wait_send()
        onward(owner, 1).wait_send()
    for copy in copies + vcopies:
        copy.wait_send()


def body(patches, vorticity, pair_source, pair_offset, pair_count, neighbours):
    smem = pl.BlockSpec(memory_space=pltpu.SMEM)
    vmem = pl.BlockSpec(memory_space=pltpu.VMEM)
    out = jax.ShapeDtypeStruct((1, COMPONENTS, SLAB, CELL * CELL), F32)
    return pl.pallas_call(
        functools.partial(kernel, patches),
        out_shape=(out, out),
        in_specs=[smem, smem, smem, smem, vmem],
        out_specs=(vmem, vmem),
        scratch_shapes=[
            pltpu.VMEM((3, PATCH_ROWS, TILE), BF16),
            pltpu.VMEM((3 * TERMS, TILE, TILE), BF16),
            pltpu.VMEM((3 * TERMS, TILE, TILE), BF16),
            pltpu.VMEM((3, HALO, 128), BF16),
            pltpu.VMEM((12, 128, TILE), BF16),
            pltpu.VMEM((12, HALO, TILE), F32),
            pltpu.VMEM((3, 12, 8, 128), F32),
            pltpu.VMEM((3, 11, 8, 128), F32),
            pltpu.SemaphoreType.DMA((3,)),
            pltpu.SemaphoreType.DMA((2 * MEMBERS,)),
            pltpu.SemaphoreType.DMA((3 * MEMBERS,)),
            pltpu.SemaphoreType.DMA((2,)),
            pltpu.SemaphoreType.DMA((2,)),
            pltpu.SemaphoreType.DMA((2,)),
            pltpu.SemaphoreType.DMA((2,)),
        ],
        compiler_params=pltpu.CompilerParams(
            collective_id=0, has_side_effects=True, vmem_limit_bytes=40 * 1024 * 1024
        ),
    )(pair_source, pair_offset, pair_count, neighbours, vorticity)


def solution(mesh):
    return jax.shard_map(
        functools.partial(body, mesh.shape["patch"]),
        mesh=mesh,
        in_specs=(
            P("patch", None, "comp", None),
            P("patch", None),
            P("patch", None),
            P("patch"),
            P("patch", None),
        ),
        out_specs=(P("patch", None, "comp", None), P("patch", None, "comp", None)),
        check_vma=False,
    )
```

time: 205 us -> 35 us (0.17)
  the two profiles are of different devices: /device:TPU:32 before, /device:TPU:6 now
where the time goes in v1:
time: 35 us; the launch traced here: 34.8 us
  Pallas kernels  31.4 us (90%)
  local copies, waits for them, and re-layouts  2.09 us (6%)
  between operations  1.37 us (4%)
    pallas_call x1, Pallas kernels, body(): pl.pallas_call(functools.partial(kernel, patches), out_shape=(out, out),...  31.4 us
    unnamed x10, local copies, waits for them, and re-layouts  2.09 us

profile of v1, /device:TPU:6, one launch (start us, length us, event | category | flops | bytes accessed | tf_op | source)
XLA Modules:
  0.0 34.8 jit_solution(13372931408113593131)
XLA Ops:
  0.6 0.0 copy-start.3
  0.6 0.0 copy-start.2
  0.7 0.0 copy-start.1
  1.3 0.0 copy-done.3
  1.3 0.0 copy-done.2
  1.4 0.0 copy-done.1
  1.4 0.0 copy-start
  1.4 0.8 %copy-done = bf16[1,3,8,1024]{3,2,1,0:T(8,128)(2,1)S(1)} copy-done((bf16[1,3,8,1024]{3,2,1,0:T(8,128)(2,1)S(1)}, bf16[1,3,8,1024]{3,2,1,0:T(8,128)(2,1)}, u32[]{:S(2)}) %copy-start) | copy-done | bytes 49176
  2.2 31.4 %shard_map.68 = (f32[1,3,8,1024]{3,2,1,0:T(8,128)S(1)}, f32[1,3,8,1024]{3,2,1,0:T(8,128)S(1)}) custom-call(s32[1,3]{1,0:T(1,128)S(1)} %copy-done.1, s32[1,3]{1,0:T(1,128)S(1)} %copy-done.2, s32[1]{0:T(128)S(6)} %copy.9.cnt_ref, s32[1,6]{1,0:T(1,128)S(1)} %copy-done.3, bf16[1,3,8,1024]{3,2,1,0:T(8,128)(2,1)S(1)} %copy-done), custom_call_target="tpu_custom_call" | custom-call | tf_op jit(solution)/shard_map/pallas_call | solution.py:414
  33.5 0.6 %copy.10 = f32[1,3,8,1024]{3,2,1,0:T(8,128)} copy(f32[1,3,8,1024]{3,2,1,0:T(8,128)S(1)} %get-tuple-element.4) | data formatting | bytes 196608
  34.2 0.6 %copy.11 = f32[1,3,8,1024]{3,2,1,0:T(8,128)} copy(f32[1,3,8,1024]{3,2,1,0:T(8,128)S(1)} %get-tuple-element.5) | data formatting | bytes 196608
Async XLA Ops:
  0.6 0.7 %copy-start.3 = (s32[1,6]{1,0:T(1,128)S(1)}, s32[1,6]{1,0:T(1,128)}, u32[]{:S(2)}) copy-start(s32[1,6]{1,0:T(1,128)} %nb_ref.1) | copy-start | bytes 76
  0.6 0.7 %copy-start.2 = (s32[1,3]{1,0:T(1,128)S(1)}, s32[1,3]{1,0:T(1,128)}, u32[]{:S(2)}) copy-start(s32[1,3]{1,0:T(1,128)} %off_ref.1) | copy-start | bytes 40
  0.7 0.7 %copy-start.1 = (s32[1,3]{1,0:T(1,128)S(1)}, s32[1,3]{1,0:T(1,128)}, u32[]{:S(2)}) copy-start(s32[1,3]{1,0:T(1,128)} %src_ref.1) | copy-start | bytes 40
  1.4 0.8 %copy-start = (bf16[1,3,8,1024]{3,2,1,0:T(8,128)(2,1)S(1)}, bf16[1,3,8,1024]{3,2,1,0:T(8,128)(2,1)}, u32[]{:S(2)}) copy-start(bf16[1,3,8,1024]{3,2,1,0:T(8,128)(2,1)} %vort_ref.1) | copy-start | bytes 147460

commit v2 on v1

--- a/solution.py
+++ b/solution.py
@@ -21,6 +21,9 @@
 F32 = jnp.float32
 BF16 = jnp.bfloat16
 MESH_ID = pl.DeviceIdType.MESH
+STEPS = (0, 1, 3, 2)
+SLOT = {step: slot for slot, step in enumerate(STEPS)}
+PARTS = (1, 1, 2)
 
 
 def iota(shape, dim):
@@ -40,12 +43,12 @@
     return pltpu.roll(grouped, shift, 1).reshape(values.shape)
 
 
-def slot_of(position, src_ref, off_ref, cnt_ref, patch):
+def slot_of(source, src_ref, off_ref, cnt_ref):
     code = jnp.int32(13)
     live = jnp.int32(0)
     count = cnt_ref[0]
     for j in range(NEAR):
-        hit = (count > j) & (src_ref[0, j] == patch - 1 + position)
+        hit = (count > j) & (src_ref[0, j] == source)
         code = jnp.where(hit, off_ref[0, j], code)
         live = jnp.where(hit, 1, live)
     shifts = (lax.div(code, 9) - 1, lax.rem(lax.div(code, 3), 3) - 1, lax.rem(code, 3) - 1)
@@ -79,18 +82,30 @@
     row = iota((HALO, 128), 0)
     col = iota((HALO, 128), 1)
     plane = (SLAB * member + jnp.where(row < 12, row, row - HALO)) & (CELL - 1)
-    term = col >> 5
+    if PARTS[position] == 1:
+        term = col >> 5
+        slot = (col >> 3) & 3
+    else:
+        term = (col >> 4) & 3
+        slot = 2 * (col >> 6) + ((col >> 3) & 1)
+    step = slot ^ (slot >> 1)
+    source = SLAB * ((member + step) & 3) + (col & 7)
     scale = jnp.where(term == 0, 1.0, jnp.where(term == 1, 1 / 16, jnp.where(term == 2, 1 / 256, 1 / 4096)))
     weight = jnp.where(term == 0, 1.0, jnp.where(term == 1, 0.5, jnp.where(term == 2, 0.25, 0.125)))
-    table = gauss(plane - (col & (CELL - 1)) - CELL * shift_x, scale).astype(BF16).astype(F32)
+    table = gauss(plane - source - CELL * shift_x, scale).astype(BF16).astype(F32)
     lx_ref[position] = (table * weight * live.astype(F32)).astype(BF16)
 
 
-def pair_products(position, gbuf, wz_ref, wy_ref, lx_ref, rbuf, acc, first):
-    lower = iota((MEMBERS, 24, 128), 2) < 64
+def zy_products(position, part, gbuf, wz_ref, wy_ref, rbuf):
+    slots = MEMBERS // PARTS[position]
+    rows = slots * CHUNK
+    lower = iota((slots, 24, 128), 2) < 64
     for k in range(TERMS):
-        along_z = jnp.dot(gbuf[position], wz_ref[position * TERMS + k], preferred_element_type=F32)
-        along_z = along_z.reshape(MEMBERS, 4, 24, TILE)
+        along_z = jnp.dot(
+            gbuf[position, part * rows : part * rows + rows],
+            wz_ref[position * TERMS + k],
+            preferred_element_type=F32,
+        ).reshape(slots, 4, 24, TILE)
         blocks = [[None] * 2 for _ in range(4)]
         for pair in range(2):
             for half in range(2):
@@ -102,10 +117,14 @@
         for block in blocks:
             joined = jnp.concatenate(block, axis=2)
             for i in range(COMPONENTS):
-                pieces.append(joined[:, 8 * i : 8 * i + 8].reshape(CELL, TILE))
+                pieces.append(joined[:, 8 * i : 8 * i + 8].reshape(8 * slots, TILE))
         swapped = jnp.concatenate(pieces, axis=0).astype(BF16)
         along_y = jnp.dot(swapped, wy_ref[position * TERMS + k], preferred_element_type=F32).astype(BF16)
-        rbuf[:, CELL * k : CELL * k + CELL, :] = along_y.reshape(12, CELL, TILE)
+        at = (part * TERMS + k) * 8 * slots
+        rbuf[:, at : at + 8 * slots, :] = along_y.reshape(12, 8 * slots, TILE)
+
+
+def x_products(position, lx_ref, rbuf, acc, first):
     for block in range(12):
         term = jnp.dot(lx_ref[position], rbuf[block], preferred_element_type=F32)
         acc[block] = term if first else acc[block] + term
@@ -242,88 +261,114 @@
     return halves(field)[0].reshape(64, 128)
 
 
-def kernel(patches, src_ref, off_ref, cnt_ref, nb_ref, vort_ref, vel_ref, str_ref,
+def kernel(patches, src_hbm, off_hbm, cnt_hbm, nb_hbm, vort_hbm, out_ref,
+           src_ref, off_ref, cnt_ref, nb_ref, vort_ref,
            gbuf, wz_ref, wy_ref, lx_ref, rbuf, acc, pbuf, vbuf,
-           xsend, fsend, grecv, psend, precv, vsend, vrecv):
+           isem, xsend, msend, csend, grecv, psend, precv, vsend, vrecv):
     patch = lax.axis_index("patch")
     member = lax.axis_index("comp")
-    left = lax.rem(patch + patches - 1, patches)
-    right = lax.rem(patch + 1, patches)
-
-    def chunk(position, owner):
-        return gbuf.at[position, pl.ds(pl.multiple_of(owner * CHUNK, CHUNK), CHUNK)]
+    odd = lax.rem(patch, 2)
+    mate = patch + 1 - 2 * odd
+    cross = lax.rem(patch + patches - 1 + 2 * odd, patches)
+    places = (patch, mate, cross)
+
+    def chunk(position, step):
+        return gbuf.at[position, pl.ds(SLOT[step % MEMBERS] * CHUNK, CHUNK)]
 
     def other(step):
         return lax.rem(member + step, MEMBERS)
 
     barrier = pltpu.get_barrier_semaphore()
-    partners = [(patch, other(d)) for d in (1, 2, 3)] + [(left, member), (right, member)]
+    partners = (
+        [(cross, member)] + [(patch, other(step)) for step in STEPS[1:]] + [(mate, member)]
+    )
     for partner in partners:
         pl.semaphore_signal(barrier, inc=1, device_id=partner, device_id_type=MESH_ID)
 
+    inputs = ((vort_hbm, vort_ref), (src_hbm, src_ref), (off_hbm, off_ref), (cnt_hbm, cnt_ref), (nb_hbm, nb_ref))
+    loads = [pltpu.make_async_copy(a, b, isem.at[n]) for n, (a, b) in enumerate(inputs)]
+    for load in loads:
+        load.start()
+    loads[0].wait()
     cells = [vort_ref[0, i].astype(F32) for i in range(COMPONENTS)]
     staged = jnp.concatenate(
         [cells[i][:, TILE * q : TILE * q + TILE] for q in range(4) for i in range(COMPONENTS)], axis=0
     ).astype(BF16)
-    gbuf[1, pl.ds(pl.multiple_of(member * CHUNK, CHUNK), CHUNK), :] = staged
+    gbuf[0, :CHUNK, :] = staged
     pl.semaphore_wait(barrier, len(partners))
 
+    def send(position, step, target, place, landing, send_sem):
+        return pltpu.make_async_remote_copy(
+            src_ref=chunk(position, step), dst_ref=chunk(place, landing),
+            send_sem=send_sem, recv_sem=grecv.at[place * MEMBERS + SLOT[landing % MEMBERS]],
+            device_id=target, device_id_type=MESH_ID,
+        )
+
     def across(step):
-        return pltpu.make_async_remote_copy(
-            src_ref=chunk(1, member), dst_ref=chunk(1, member),
-            send_sem=xsend.at[step - 1], recv_sem=grecv.at[MEMBERS + member],
-            device_id=(patch, other(step)), device_id_type=MESH_ID,
-        )
-
-    def onward(owner, step):
-        target, place = ((right, 0), (left, 2))[step]
-        return pltpu.make_async_remote_copy(
-            src_ref=chunk(1, owner), dst_ref=chunk(place, owner),
-            send_sem=fsend.at[2 * owner + step], recv_sem=grecv.at[place * MEMBERS + owner],
-            device_id=(target, member), device_id_type=MESH_ID,
-        )
-
-    def arrived(position, owner):
+        return send(0, 0, (patch, other(step)), 0, -step, xsend.at[step - 1])
+
+    def to_mate(step):
+        return send(0, step, (mate, member), 1, step, msend.at[step])
+
+    def to_cross(step):
+        return send(0, step, (cross, member), 2, step, csend.at[step])
+
+    def opposite():
+        return send(2, 0, (patch, other(2)), 2, 2, csend.at[2])
+
+    def arrived(position, step):
         pltpu.make_async_remote_copy(
-            src_ref=chunk(position, owner), dst_ref=chunk(position, owner),
-            send_sem=xsend.at[0], recv_sem=grecv.at[position * MEMBERS + owner],
-            device_id=(right, member), device_id_type=MESH_ID,
+            src_ref=chunk(position, step), dst_ref=chunk(position, step),
+            send_sem=xsend.at[0], recv_sem=grecv.at[position * MEMBERS + SLOT[step]],
+            device_id=(cross, member), device_id_type=MESH_ID,
         ).wait_recv()
 
-    across(1).start()
-    across(3).start()
-    onward(member, 0).start()
-    onward(member, 1).start()
-    across(2).start()
+    started = []
+
+    def start(copy):
+        copy.start()
+        started.append(copy)
+
+    for copy in (across(1), across(3), to_cross(0), to_mate(0), across(2)):
+        start(copy)
+    for load in loads[1:]:
+        load.wait()
 
     def tables(position):
-        shifts, live = slot_of(position, src_ref, off_ref, cnt_ref, patch)
+        shifts, live = slot_of(places[position], src_ref, off_ref, cnt_ref)
         write_tables(position, shifts, live, member, wz_ref, wy_ref, lx_ref)
 
-    def products(position, first):
-        pair_products(position, gbuf, wz_ref, wy_ref, lx_ref, rbuf, acc, first)
-
+    def products(position, waiting, first):
+        rows = len(STEPS) // PARTS[position]
+        for part in range(PARTS[position]):
+            for step in STEPS[part * rows : part * rows + rows]:
+                if step in waiting:
+                    arrived(position, step)
+            zy_products(position, part, gbuf, wz_ref, wy_ref, rbuf)
+        x_products(position, lx_ref, rbuf, acc, first)
+
+    tables(0)
+    for step in (1, 3):
+        arrived(0, step)
+        start(to_cross(step))
+        start(to_mate(step))
+    arrived(2, 0)
+    start(opposite())
+    arrived(0, 2)
+    start(to_mate(2))
     tables(1)
-    for step in (1, 3, 2):
-        owner = other(step)
-        arrived(1, owner)
-        onward(owner, 0).start()
-        onward(owner, 1).start()
-    tables(0)
     tables(2)
-    products(1, True)
-    for position in (0, 2):
-        for step in (0, 1, 3, 2):
-            arrived(position, other(step))
-        products(position, False)
+    products(0, (), True)
+    products(1, STEPS, False)
+    products(2, STEPS[1:], False)
 
     def exchange(buffer, send, recv):
         copies = []
-        for step, (target, place) in enumerate(((right, 0), (left, 2))):
+        for step, place in ((1, 2), (0, 1)):
             copies.append(pltpu.make_async_remote_copy(
-                src_ref=buffer.at[1], dst_ref=buffer.at[place],
+                src_ref=buffer.at[0], dst_ref=buffer.at[place],
                 send_sem=send.at[step], recv_sem=recv.at[step],
-                device_id=(target, member), device_id_type=MESH_ID,
+                device_id=(places[place], member), device_id_type=MESH_ID,
             ))
         for copy in copies:
             copy.start()
@@ -332,7 +377,7 @@
     def pick(buffer, face, index, shape):
         source = jnp.full(shape, nb_ref[0, face], jnp.int32)
         parts = [buffer[place, index].reshape(shape) for place in range(3)]
-        chosen = jnp.where(source < patch, parts[0], jnp.where(source == patch, parts[1], parts[2]))
+        chosen = jnp.where(source == patch, parts[0], jnp.where(source == mate, parts[1], parts[2]))
         return jnp.where(source < 0, 0.0, chosen)
 
     def ghosts(buffer, rows, z_count, y_count, x_count):
@@ -359,9 +404,9 @@
     px, py, pz = potential_of(acc)
     packs = pack_z([px, py], HALO) + [pack_y(px, HALO), pack_y(pz, HALO)]
     for index, part in enumerate(packs):
-        pbuf[1, 2 * index : 2 * index + 2] = part.reshape(2, 8, 128)
+        pbuf[0, 2 * index : 2 * index + 2] = part.reshape(2, 8, 128)
     for index, part in enumerate(pack_x([py, pz], member)):
-        pbuf[1, 8 + 2 * index : 10 + 2 * index] = part
+        pbuf[0, 8 + 2 * index : 10 + 2 * index] = part
     copies = exchange(pbuf, psend, precv)
     for copy in copies:
         copy.wait_recv()
@@ -374,13 +419,13 @@
     own = [own_rows(v) for v in velocity]
     packs = pack_z(own, 8) + [pack_y(v, 8) for v in own]
     for index, part in enumerate(packs):
-        vbuf[1, index] = part
+        vbuf[0, index] = part
     for index, part in enumerate(pack_x(velocity, member)):
-        vbuf[1, 5 + 2 * index : 7 + 2 * index] = part
+        vbuf[0, 5 + 2 * index : 7 + 2 * index] = part
     vcopies = exchange(vbuf, vsend, vrecv)
     for i in range(COMPONENTS):
         for v in range(8):
-            vel_ref[0, i, :, 128 * v : 128 * v + 128] = own[i][8 * v : 8 * v + 8]
+            out_ref[0, i, :, 128 * v : 128 * v + 128] = own[i][8 * v : 8 * v + 8]
     for copy in vcopies:
         copy.wait_recv()
     zs, ys, xs = ghosts(vbuf, 8, 3, 3, 3)
@@ -396,27 +441,27 @@
             + spin[2] * grad_z(own[i], above[i], below[i])
         )
         for v in range(8):
-            str_ref[0, i, :, 128 * v : 128 * v + 128] = total[8 * v : 8 * v + 8]
-
-    for step in (1, 2, 3):
-        across(step).wait_send()
-    for owner in range(MEMBERS):
-        onward(owner, 0).wait_send()
-        onward(owner, 1).wait_send()
-    for copy in copies + vcopies:
+            out_ref[0, 3 + i, :, 128 * v : 128 * v + 128] = total[8 * v : 8 * v + 8]
+
+    for copy in started + copies + vcopies:
         copy.wait_send()
 
 
 def body(patches, vorticity, pair_source, pair_offset, pair_count, neighbours):
-    smem = pl.BlockSpec(memory_space=pltpu.SMEM)
+    hbm = pl.BlockSpec(memory_space=pltpu.HBM)
     vmem = pl.BlockSpec(memory_space=pltpu.VMEM)
-    out = jax.ShapeDtypeStruct((1, COMPONENTS, SLAB, CELL * CELL), F32)
-    return pl.pallas_call(
+    out = jax.ShapeDtypeStruct((1, 2 * COMPONENTS, SLAB, CELL * CELL), F32)
+    both = pl.pallas_call(
         functools.partial(kernel, patches),
-        out_shape=(out, out),
-        in_specs=[smem, smem, smem, smem, vmem],
-        out_specs=(vmem, vmem),
+        out_shape=out,
+        in_specs=[hbm] * 5,
+        out_specs=vmem,
         scratch_shapes=[
+            pltpu.SMEM((1, NEAR), jnp.int32),
+            pltpu.SMEM((1, NEAR), jnp.int32),
+            pltpu.SMEM((1,), jnp.int32),
+            pltpu.SMEM((1, 6), jnp.int32),
+            pltpu.VMEM((1, COMPONENTS, SLAB, CELL * CELL), BF16),
             pltpu.VMEM((3, PATCH_ROWS, TILE), BF16),
             pltpu.VMEM((3 * TERMS, TILE, TILE), BF16),
             pltpu.VMEM((3 * TERMS, TILE, TILE), BF16),
@@ -425,7 +470,9 @@
             pltpu.VMEM((12, HALO, TILE), F32),
             pltpu.VMEM((3, 12, 8, 128), F32),
             pltpu.VMEM((3, 11, 8, 128), F32),
+            pltpu.SemaphoreType.DMA((5,)),
             pltpu.SemaphoreType.DMA((3,)),
+            pltpu.SemaphoreType.DMA((MEMBERS,)),
             pltpu.SemaphoreType.DMA((2 * MEMBERS,)),
             pltpu.SemaphoreType.DMA((3 * MEMBERS,)),
             pltpu.SemaphoreType.DMA((2,)),
@@ -434,9 +481,10 @@
             pltpu.SemaphoreType.DMA((2,)),
         ],
         compiler_params=pltpu.CompilerParams(
-            collective_id=0, has_side_effects=True, vmem_limit_bytes=40 * 1024 * 1024
+            collective_id=0, has_side_effects=True, vmem_limit_bytes=40 << 20
         ),
     )(pair_source, pair_offset, pair_count, neighbours, vorticity)
+    return both[:, :3], both[:, 3:]
 
 
 def solution(mesh):

time: 35 us -> 33 us (0.943)
  the two profiles are of different devices: /device:TPU:6 before, /device:TPU:4 now
where the time goes in v2:
time: 33 us; the launch traced here: 32.8 us
  Pallas kernels  29.9 us (91%)
  local copies, waits for them, and re-layouts  1.49 us (5%)
  between operations  1.36 us (4%)
    pallas_call x1, Pallas kernels, body(): pl.pallas_call(functools.partial(kernel, patches), out_shape=out, in_spec...  29.9 us
    unnamed x8, local copies, waits for them, and re-layouts  0.8 us
    slice x1, local copies, waits for them, and re-layouts, body(): return (both[:, :3], both[:, 3:])  0.69 us

profile of v2, /device:TPU:4, one launch (start us, length us, event | category | flops | bytes accessed | tf_op | source)
XLA Modules:
  0.0 32.8 jit_solution(16269535585405687896)
XLA Ops:
  0.6 0.0 copy-start.3
  0.6 0.0 copy-start.2
  0.7 0.0 copy-start.1
  1.3 0.0 copy-done.3
  1.3 0.0 copy-done.2
  1.4 0.0 copy-done.1
  1.4 0.0 copy-start
  1.4 0.8 %copy-done = bf16[1,3,8,1024]{3,2,1,0:T(8,128)(2,1)S(1)} copy-done((bf16[1,3,8,1024]{3,2,1,0:T(8,128)(2,1)S(1)}, bf16[1,3,8,1024]{3,2,1,0:T(8,128)(2,1)}, u32[]{:S(2)}) %copy-start) | copy-done | bytes 49176
  2.2 29.9 %shard_map.68 = f32[1,6,8,1024]{3,2,1,0:T(8,128)S(1)} custom-call(s32[1,3]{1,0:T(1,128)S(1)} %copy-done.1, s32[1,3]{1,0:T(1,128)S(1)} %copy-done.2, s32[1]{0:T(128)S(6)} %copy.7.cnt_hbm, s32[1,6]{1,0:T(1,128)S(1)} %copy-done.3, bf16[1,3,8,1024]{3,2,1,0:T(8,128)(2,1)S(1)} %copy-done), custom_call_target="tpu_custom_call" | custom-call | tf_op jit(solution)/shard_map/pallas_call | solution.py:454
  32.1 0.7 %fusion = (f32[1,3,8,1024]{3,2,1,0:T(8,128)}, f32[1,3,8,1024]{3,2,1,0:T(8,128)}) fusion(f32[1,6,8,1024]{3,2,1,0:T(8,128)S(1)} %shard_map.68), kind=kLoop, calls=%fused_computation | loop fusion | bytes 393216 | tf_op jit(solution)/shard_map/slice | solution.py:487
Async XLA Ops:
  0.6 0.7 %copy-start.3 = (s32[1,6]{1,0:T(1,128)S(1)}, s32[1,6]{1,0:T(1,128)}, u32[]{:S(2)}) copy-start(s32[1,6]{1,0:T(1,128)} %nb_hbm.1) | copy-start | bytes 76
  0.6 0.7 %copy-start.2 = (s32[1,3]{1,0:T(1,128)S(1)}, s32[1,3]{1,0:T(1,128)}, u32[]{:S(2)}) copy-start(s32[1,3]{1,0:T(1,128)} %off_hbm.1) | copy-start | bytes 40
  0.7 0.7 %copy-start.1 = (s32[1,3]{1,0:T(1,128)S(1)}, s32[1,3]{1,0:T(1,128)}, u32[]{:S(2)}) copy-start(s32[1,3]{1,0:T(1,128)} %src_hbm.1) | copy-start | bytes 40
  1.4 0.8 %copy-start = (bf16[1,3,8,1024]{3,2,1,0:T(8,128)(2,1)S(1)}, bf16[1,3,8,1024]{3,2,1,0:T(8,128)(2,1)}, u32[]{:S(2)}) copy-start(bf16[1,3,8,1024]{3,2,1,0:T(8,128)(2,1)} %vort_hbm.1) | copy-start | bytes 147460

commit v3 on v2

--- a/solution.py
+++ b/solution.py
@@ -23,6 +23,7 @@
 MESH_ID = pl.DeviceIdType.MESH
 STEPS = (0, 1, 3, 2)
 SLOT = {step: slot for slot, step in enumerate(STEPS)}
+PIECES = 1
 PARTS = (1, 1, 2)
 
 
@@ -271,19 +272,27 @@
     mate = patch + 1 - 2 * odd
     cross = lax.rem(patch + patches - 1 + 2 * odd, patches)
     places = (patch, mate, cross)
-
-    def chunk(position, step):
-        return gbuf.at[position, pl.ds(SLOT[step % MEMBERS] * CHUNK, CHUNK)]
+    inner = (patch > 0) & (patch < patches - 1)
+
+    def chunk(position, step, piece):
+        rows = CHUNK // PIECES
+        return gbuf.at[position, pl.ds(SLOT[step % MEMBERS] * CHUNK + piece * rows, rows)]
 
     def other(step):
         return lax.rem(member + step, MEMBERS)
 
     barrier = pltpu.get_barrier_semaphore()
-    partners = (
-        [(cross, member)] + [(patch, other(step)) for step in STEPS[1:]] + [(mate, member)]
-    )
-    for partner in partners:
+
+    def greet(partner):
         pl.semaphore_signal(barrier, inc=1, device_id=partner, device_id_type=MESH_ID)
+
+    @pl.when(inner)
+    def _():
+        greet((cross, member))
+
+    for step in STEPS[1:]:
+        greet((patch, other(step)))
+    greet((mate, member))
 
     inputs = ((vort_hbm, vort_ref), (src_hbm, src_ref), (off_hbm, off_ref), (cnt_hbm, cnt_ref), (nb_hbm, nb_ref))
     loads = [pltpu.make_async_copy(a, b, isem.at[n]) for n, (a, b) in enumerate(inputs)]
@@ -295,42 +304,48 @@
         [cells[i][:, TILE * q : TILE * q + TILE] for q in range(4) for i in range(COMPONENTS)], axis=0
     ).astype(BF16)
     gbuf[0, :CHUNK, :] = staged
-    pl.semaphore_wait(barrier, len(partners))
-
-    def send(position, step, target, place, landing, send_sem):
+    pl.semaphore_wait(barrier, jnp.where(inner, 5, 4))
+
+    def send(position, step, piece, target, place, landing, send_sem):
         return pltpu.make_async_remote_copy(
-            src_ref=chunk(position, step), dst_ref=chunk(place, landing),
-            send_sem=send_sem, recv_sem=grecv.at[place * MEMBERS + SLOT[landing % MEMBERS]],
+            src_ref=chunk(position, step, piece), dst_ref=chunk(place, landing, piece),
+            send_sem=send_sem, recv_sem=grecv.at[place * MEMBERS + SLOT[landing % MEMBERS], piece],
             device_id=target, device_id_type=MESH_ID,
         )
 
-    def across(step):
-        return send(0, 0, (patch, other(step)), 0, -step, xsend.at[step - 1])
-
-    def to_mate(step):
-        return send(0, step, (mate, member), 1, step, msend.at[step])
-
-    def to_cross(step):
-        return send(0, step, (cross, member), 2, step, csend.at[step])
-
-    def opposite():
-        return send(2, 0, (patch, other(2)), 2, 2, csend.at[2])
-
-    def arrived(position, step):
+    def across(step, piece):
+        return send(0, 0, piece, (patch, other(step)), 0, -step, xsend.at[step - 1, piece])
+
+    def to_mate(step, piece):
+        return send(0, step, piece, (mate, member), 1, step, msend.at[step, piece])
+
+    def to_cross(step, piece):
+        return send(0, step, piece, (cross, member), 2, step, csend.at[step, piece])
+
+    def opposite(piece):
+        return send(2, 0, piece, (patch, other(2)), 2, 2, csend.at[2, piece])
+
+    def arrived(position, step, piece):
         pltpu.make_async_remote_copy(
-            src_ref=chunk(position, step), dst_ref=chunk(position, step),
-            send_sem=xsend.at[0], recv_sem=grecv.at[position * MEMBERS + SLOT[step]],
+            src_ref=chunk(position, step, piece), dst_ref=chunk(position, step, piece),
+            send_sem=xsend.at[0, 0], recv_sem=grecv.at[position * MEMBERS + SLOT[step], piece],
             device_id=(cross, member), device_id_type=MESH_ID,
         ).wait_recv()
 
-    started = []
-
-    def start(copy):
-        copy.start()
-        started.append(copy)
-
-    for copy in (across(1), across(3), to_cross(0), to_mate(0), across(2)):
-        start(copy)
+    pieces = range(PIECES)
+    for step in (1, 3):
+        for piece in pieces:
+            across(step, piece).start()
+
+    @pl.when(inner)
+    def _():
+        for piece in pieces:
+            to_cross(0, piece).start()
+
+    for piece in pieces:
+        to_mate(0, piece).start()
+    for piece in pieces:
+        across(2, piece).start()
     for load in loads[1:]:
         load.wait()
 
@@ -342,37 +357,61 @@
         rows = len(STEPS) // PARTS[position]
         for part in range(PARTS[position]):
             for step in STEPS[part * rows : part * rows + rows]:
-                if step in waiting:
-                    arrived(position, step)
+                for piece in pieces if step in waiting else ():
+                    arrived(position, step, piece)
             zy_products(position, part, gbuf, wz_ref, wy_ref, rbuf)
         x_products(position, lx_ref, rbuf, acc, first)
 
     tables(0)
-    for step in (1, 3):
-        arrived(0, step)
-        start(to_cross(step))
-        start(to_mate(step))
-    arrived(2, 0)
-    start(opposite())
-    arrived(0, 2)
-    start(to_mate(2))
+    for piece in pieces:
+        for step in (1, 3):
+            arrived(0, step, piece)
+
+            @pl.when(inner)
+            def _():
+                to_cross(step, piece).start()
+
+            to_mate(step, piece).start()
+
+    @pl.when(inner)
+    def _():
+        for piece in pieces:
+            arrived(2, 0, piece)
+            opposite(piece).start()
+
+    for piece in pieces:
+        arrived(0, 2, piece)
+        to_mate(2, piece).start()
     tables(1)
     tables(2)
     products(0, (), True)
     products(1, STEPS, False)
-    products(2, STEPS[1:], False)
+
+    @pl.when(inner)
+    def _():
+        products(2, STEPS[1:], False)
+
+    @pl.when(jnp.logical_not(inner))
+    def _():
+        pbuf[2] = jnp.zeros(pbuf.shape[1:], F32)
+        vbuf[2] = jnp.zeros(vbuf.shape[1:], F32)
 
     def exchange(buffer, send, recv):
-        copies = []
-        for step, place in ((1, 2), (0, 1)):
-            copies.append(pltpu.make_async_remote_copy(
+        return [
+            pltpu.make_async_remote_copy(
                 src_ref=buffer.at[0], dst_ref=buffer.at[place],
-                send_sem=send.at[step], recv_sem=recv.at[step],
+                send_sem=send.at[place - 1], recv_sem=recv.at[place - 1],
                 device_id=(places[place], member), device_id_type=MESH_ID,
-            ))
-        for copy in copies:
-            copy.start()
-        return copies
+            )
+            for place in (2, 1)
+        ]
+
+    def act(copies, name):
+        @pl.when(inner)
+        def _():
+            getattr(copies[0], name)()
+
+        getattr(copies[1], name)()
 
     def pick(buffer, face, index, shape):
         source = jnp.full(shape, nb_ref[0, face], jnp.int32)
@@ -408,8 +447,8 @@
     for index, part in enumerate(pack_x([py, pz], member)):
         pbuf[0, 8 + 2 * index : 10 + 2 * index] = part
     copies = exchange(pbuf, psend, precv)
-    for copy in copies:
-        copy.wait_recv()
+    act(copies, "start")
+    act(copies, "wait_recv")
     zs, ys, xs = ghosts(pbuf, HALO, 2, 2, 2)
     above, below = unpack_z(zs, 2, HALO)
     vx = grad_y(pz, ys[1], HALO) - grad_z(py, above[1], below[1])
@@ -423,11 +462,11 @@
     for index, part in enumerate(pack_x(velocity, member)):
         vbuf[0, 5 + 2 * index : 7 + 2 * index] = part
     vcopies = exchange(vbuf, vsend, vrecv)
+    act(vcopies, "start")
     for i in range(COMPONENTS):
         for v in range(8):
             out_ref[0, i, :, 128 * v : 128 * v + 128] = own[i][8 * v : 8 * v + 8]
-    for copy in vcopies:
-        copy.wait_recv()
+    act(vcopies, "wait_recv")
     zs, ys, xs = ghosts(vbuf, 8, 3, 3, 3)
     above, below = unpack_z(zs, 3, 8)
     spin = [
@@ -443,8 +482,21 @@
         for v in range(8):
             out_ref[0, 3 + i, :, 128 * v : 128 * v + 128] = total[8 * v : 8 * v + 8]
 
-    for copy in started + copies + vcopies:
-        copy.wait_send()
+    for piece in pieces:
+        for step in (1, 2, 3):
+            across(step, piece).wait_send()
+        for step in STEPS:
+            to_mate(step, piece).wait_send()
+
+    @pl.when(inner)
+    def _():
+        for piece in pieces:
+            for step in (0, 1, 3):
+                to_cross(step, piece).wait_send()
+            opposite(piece).wait_send()
+
+    act(copies, "wait_send")
+    act(vcopies, "wait_send")
 
 
 def body(patches, vorticity, pair_source, pair_offset, pair_count, neighbours):
@@ -471,10 +523,10 @@
             pltpu.VMEM((3, 12, 8, 128), F32),
             pltpu.VMEM((3, 11, 8, 128), F32),
             pltpu.SemaphoreType.DMA((5,)),
-            pltpu.SemaphoreType.DMA((3,)),
-            pltpu.SemaphoreType.DMA((MEMBERS,)),
-            pltpu.SemaphoreType.DMA((2 * MEMBERS,)),
-            pltpu.SemaphoreType.DMA((3 * MEMBERS,)),
+            pltpu.SemaphoreType.DMA((3, PIECES)),
+            pltpu.SemaphoreType.DMA((MEMBERS, PIECES)),
+            pltpu.SemaphoreType.DMA((MEMBERS, PIECES)),
+            pltpu.SemaphoreType.DMA((3 * MEMBERS, PIECES)),
             pltpu.SemaphoreType.DMA((2,)),
             pltpu.SemaphoreType.DMA((2,)),
             pltpu.SemaphoreType.DMA((2,)),

time: 33 us -> 30.9 us (0.936)
  the two profiles are of different devices: /device:TPU:4 before, /device:TPU:32 now
where the time goes in v3:
time: 30.9 us; the launch traced here: 30.7 us
  Pallas kernels  27.9 us (90%)
  local copies, waits for them, and re-layouts  1.49 us (5%)
  between operations  1.36 us (4%)
    pallas_call x1, Pallas kernels, body(): pl.pallas_call(functools.partial(kernel, patches), out_shape=out, in_spec...  27.9 us
    unnamed x8, local copies, waits for them, and re-layouts  0.8 us
    slice x1, local copies, waits for them, and re-layouts, body(): return (both[:, :3], both[:, 3:])  0.69 us

profile of v3, /device:TPU:32, one launch (start us, length us, event | category | flops | bytes accessed | tf_op | source)
XLA Modules:
  0.0 30.7 jit_solution(3733988209492904872)
XLA Ops:
  0.6 0.0 copy-start.3
  0.6 0.0 copy-start.2
  0.7 0.0 copy-start.1
  1.3 0.0 copy-done.3
  1.3 0.0 copy-done.2
  1.4 0.0 copy-done.1
  1.4 0.0 copy-start
  1.4 0.8 %copy-done = bf16[1,3,8,1024]{3,2,1,0:T(8,128)(2,1)S(1)} copy-done((bf16[1,3,8,1024]{3,2,1,0:T(8,128)(2,1)S(1)}, bf16[1,3,8,1024]{3,2,1,0:T(8,128)(2,1)}, u32[]{:S(2)}) %copy-start) | copy-done | bytes 49176
  2.2 27.9 %shard_map.68 = f32[1,6,8,1024]{3,2,1,0:T(8,128)S(1)} custom-call(s32[1,3]{1,0:T(1,128)S(1)} %copy-done.1, s32[1,3]{1,0:T(1,128)S(1)} %copy-done.2, s32[1]{0:T(128)S(6)} %copy.7.cnt_hbm, s32[1,6]{1,0:T(1,128)S(1)} %copy-done.3, bf16[1,3,8,1024]{3,2,1,0:T(8,128)(2,1)S(1)} %copy-done), custom_call_target="tpu_custom_call" | custom-call | tf_op jit(solution)/shard_map/pallas_call | solution.py:506
  30.1 0.7 %fusion = (f32[1,3,8,1024]{3,2,1,0:T(8,128)}, f32[1,3,8,1024]{3,2,1,0:T(8,128)}) fusion(f32[1,6,8,1024]{3,2,1,0:T(8,128)S(1)} %shard_map.68), kind=kLoop, calls=%fused_computation | loop fusion | bytes 393216 | tf_op jit(solution)/shard_map/slice | solution.py:539
Async XLA Ops:
  0.6 0.7 %copy-start.3 = (s32[1,6]{1,0:T(1,128)S(1)}, s32[1,6]{1,0:T(1,128)}, u32[]{:S(2)}) copy-start(s32[1,6]{1,0:T(1,128)} %nb_hbm.1) | copy-start | bytes 76
  0.6 0.7 %copy-start.2 = (s32[1,3]{1,0:T(1,128)S(1)}, s32[1,3]{1,0:T(1,128)}, u32[]{:S(2)}) copy-start(s32[1,3]{1,0:T(1,128)} %off_hbm.1) | copy-start | bytes 40
  0.7 0.7 %copy-start.1 = (s32[1,3]{1,0:T(1,128)S(1)}, s32[1,3]{1,0:T(1,128)}, u32[]{:S(2)}) copy-start(s32[1,3]{1,0:T(1,128)} %src_hbm.1) | copy-start | bytes 40
  1.4 0.8 %copy-start = (bf16[1,3,8,1024]{3,2,1,0:T(8,128)(2,1)S(1)}, bf16[1,3,8,1024]{3,2,1,0:T(8,128)(2,1)}, u32[]{:S(2)}) copy-start(bf16[1,3,8,1024]{3,2,1,0:T(8,128)(2,1)} %vort_hbm.1) | copy-start | bytes 147460

commit v4 on v3

--- a/solution.py
+++ b/solution.py
@@ -24,7 +24,9 @@
 STEPS = (0, 1, 3, 2)
 SLOT = {step: slot for slot, step in enumerate(STEPS)}
 PIECES = 1
-PARTS = (1, 1, 2)
+OWN, MATE, FAR, BACK = range(4)
+SOURCES = (OWN, MATE, FAR, OWN)
+PARTS = (2, 1, 2, 1)
 
 
 def iota(shape, dim):
@@ -94,7 +96,7 @@
     scale = jnp.where(term == 0, 1.0, jnp.where(term == 1, 1 / 16, jnp.where(term == 2, 1 / 256, 1 / 4096)))
     weight = jnp.where(term == 0, 1.0, jnp.where(term == 1, 0.5, jnp.where(term == 2, 0.25, 0.125)))
     table = gauss(plane - source - CELL * shift_x, scale).astype(BF16).astype(F32)
-    lx_ref[position] = (table * weight * live.astype(F32)).astype(BF16)
+    lx_ref[position] = (table * weight * live).astype(BF16)
 
 
 def zy_products(position, part, gbuf, wz_ref, wy_ref, rbuf):
@@ -103,7 +105,7 @@
     lower = iota((slots, 24, 128), 2) < 64
     for k in range(TERMS):
         along_z = jnp.dot(
-            gbuf[position, part * rows : part * rows + rows],
+            gbuf[SOURCES[position], part * rows : part * rows + rows],
             wz_ref[position * TERMS + k],
             preferred_element_type=F32,
         ).reshape(slots, 4, 24, TILE)
@@ -125,13 +127,13 @@
         rbuf[:, at : at + 8 * slots, :] = along_y.reshape(12, 8 * slots, TILE)
 
 
-def x_products(position, lx_ref, rbuf, acc, first):
+def x_products(position, total, lx_ref, rbuf, acc, first):
     for block in range(12):
         term = jnp.dot(lx_ref[position], rbuf[block], preferred_element_type=F32)
-        acc[block] = term if first else acc[block] + term
-
-
-def potential_of(acc):
+        acc[total, block] = term if first else acc[total, block] + term
+
+
+def potential_of(acc, total):
     lane = iota((2 * HALO, 128), 1)
     bit4 = (lane & 16) == 0
     bit3 = (lane & 8) == 0
@@ -139,7 +141,7 @@
     for i in range(COMPONENTS):
         a = []
         for block in range(4):
-            tile = acc[3 * block + i] * W0
+            tile = acc[total, 3 * block + i] * W0
             a.append(jnp.concatenate([tile[:, :128], tile[:, 128:]], axis=0))
         b = [
             jnp.where(bit4, a[0], lane_roll(a[2], 16)),
@@ -264,8 +266,8 @@
 
 def kernel(patches, src_hbm, off_hbm, cnt_hbm, nb_hbm, vort_hbm, out_ref,
            src_ref, off_ref, cnt_ref, nb_ref, vort_ref,
-           gbuf, wz_ref, wy_ref, lx_ref, rbuf, acc, pbuf, vbuf,
-           isem, xsend, msend, csend, grecv, psend, precv, vsend, vrecv):
+           gbuf, wz_ref, wy_ref, lx_ref, rbuf, acc, potential, pbuf, back, vbuf, info,
+           isem, xsend, msend, csend, grecv, psend, precv, vsend, vrecv, nsend, nrecv):
     patch = lax.axis_index("patch")
     member = lax.axis_index("comp")
     odd = lax.rem(patch, 2)
@@ -351,18 +353,32 @@
 
     def tables(position):
         shifts, live = slot_of(places[position], src_ref, off_ref, cnt_ref)
-        write_tables(position, shifts, live, member, wz_ref, wy_ref, lx_ref)
-
-    def products(position, waiting, first):
+        write_tables(position, shifts, live.astype(F32), member, wz_ref, wy_ref, lx_ref)
+
+    def products(position, waiting, total, first):
         rows = len(STEPS) // PARTS[position]
         for part in range(PARTS[position]):
             for step in STEPS[part * rows : part * rows + rows]:
                 for piece in pieces if step in waiting else ():
                     arrived(position, step, piece)
             zy_products(position, part, gbuf, wz_ref, wy_ref, rbuf)
-        x_products(position, lx_ref, rbuf, acc, first)
-
-    tables(0)
+        x_products(position, total, lx_ref, rbuf, acc, first)
+
+    note = pltpu.make_async_remote_copy(
+        src_ref=info.at[0], dst_ref=info.at[1], send_sem=nsend.at[0], recv_sem=nrecv.at[0],
+        device_id=(cross, member), device_id_type=MESH_ID,
+    )
+
+    @pl.when(inner)
+    def _():
+        shifts, live = slot_of(cross, src_ref, off_ref, cnt_ref)
+        row = iota((8, TILE), 0)
+        info[0] = jnp.where(
+            row == 0, shifts[0], jnp.where(row == 1, shifts[1], jnp.where(row == 2, shifts[2], live))
+        )
+        note.start()
+
+    tables(OWN)
     for piece in pieces:
         for step in (1, 3):
             arrived(0, step, piece)
@@ -379,31 +395,23 @@
             arrived(2, 0, piece)
             opposite(piece).start()
 
+    zy_products(OWN, 0, gbuf, wz_ref, wy_ref, rbuf)
     for piece in pieces:
         arrived(0, 2, piece)
         to_mate(2, piece).start()
-    tables(1)
-    tables(2)
-    products(0, (), True)
-    products(1, STEPS, False)
-
-    @pl.when(inner)
-    def _():
-        products(2, STEPS[1:], False)
-
-    @pl.when(jnp.logical_not(inner))
-    def _():
-        pbuf[2] = jnp.zeros(pbuf.shape[1:], F32)
-        vbuf[2] = jnp.zeros(vbuf.shape[1:], F32)
-
-    def exchange(buffer, send, recv):
+    tables(MATE)
+    zy_products(OWN, 1, gbuf, wz_ref, wy_ref, rbuf)
+    x_products(OWN, 0, lx_ref, rbuf, acc, True)
+    products(MATE, STEPS, 0, False)
+
+    def exchange(buffer, places_from, send, recv):
         return [
             pltpu.make_async_remote_copy(
-                src_ref=buffer.at[0], dst_ref=buffer.at[place],
+                src_ref=buffer.at[source], dst_ref=buffer.at[place],
                 send_sem=send.at[place - 1], recv_sem=recv.at[place - 1],
                 device_id=(places[place], member), device_id_type=MESH_ID,
             )
-            for place in (2, 1)
+            for place, source in zip((FAR, MATE), places_from)
         ]
 
     def act(copies, name):
@@ -440,15 +448,58 @@
             at += 2
         return zs, ys, xs
 
-    px, py, pz = potential_of(acc)
-    packs = pack_z([px, py], HALO) + [pack_y(px, HALO), pack_y(pz, HALO)]
-    for index, part in enumerate(packs):
-        pbuf[0, 2 * index : 2 * index + 2] = part.reshape(2, 8, 128)
-    for index, part in enumerate(pack_x([py, pz], member)):
-        pbuf[0, 8 + 2 * index : 10 + 2 * index] = part
-    copies = exchange(pbuf, psend, precv)
-    act(copies, "start")
-    act(copies, "wait_recv")
+    def pack_potential(fields, store):
+        px, py, pz = fields
+        packs = pack_z([px, py], HALO) + [pack_y(px, HALO), pack_y(pz, HALO)]
+        for index, part in enumerate(packs):
+            store(pl.ds(2 * index, 2), part.reshape(2, 8, 128))
+        for index, part in enumerate(pack_x([py, pz], member)):
+            store(pl.ds(8 + 2 * index, 2), part)
+
+    def into(buffer, place):
+        def store(index, part):
+            buffer[place, index] = part
+
+        return store
+
+    copies = exchange(pbuf, (3, 0), psend, precv)
+    near = potential_of(acc, 0)
+    for i in range(COMPONENTS):
+        potential[i] = near[i]
+
+    @pl.when(inner)
+    def _():
+        pack_potential(near, into(pbuf, 3))
+        copies[0].start()
+        tables(FAR)
+        note.wait_recv()
+        sent = info[1]
+        write_tables(
+            BACK, (sent[0:1, :128], sent[1:2], sent[2:3]), sent[3:4, :128].astype(F32),
+            member, wz_ref, wy_ref, lx_ref,
+        )
+        products(BACK, (), 1, True)
+        pack_potential(potential_of(acc, 1), into(back, 0))
+        products(FAR, STEPS[1:], 2, True)
+        far = potential_of(acc, 2)
+        for i in range(COMPONENTS):
+            potential[i] = potential[i] + far[i]
+
+    @pl.when(jnp.logical_not(inner))
+    def _():
+        pbuf[FAR] = jnp.zeros(pbuf.shape[1:], F32)
+        vbuf[FAR] = jnp.zeros(vbuf.shape[1:], F32)
+
+    px, py, pz = [potential[i] for i in range(COMPONENTS)]
+    pack_potential((px, py, pz), into(pbuf, 0))
+    copies[1].start()
+
+    @pl.when(inner)
+    def _():
+        copies[0].wait_recv()
+        pbuf[FAR] = pbuf[FAR] + back[0]
+
+    copies[1].wait_recv()
     zs, ys, xs = ghosts(pbuf, HALO, 2, 2, 2)
     above, below = unpack_z(zs, 2, HALO)
     vx = grad_y(pz, ys[1], HALO) - grad_z(py, above[1], below[1])
@@ -461,7 +512,7 @@
         vbuf[0, index] = part
     for index, part in enumerate(pack_x(velocity, member)):
         vbuf[0, 5 + 2 * index : 7 + 2 * index] = part
-    vcopies = exchange(vbuf, vsend, vrecv)
+    vcopies = exchange(vbuf, (0, 0), vsend, vrecv)
     act(vcopies, "start")
     for i in range(COMPONENTS):
         for v in range(8):
@@ -495,6 +546,10 @@
                 to_cross(step, piece).wait_send()
             opposite(piece).wait_send()
 
+    @pl.when(inner)
+    def _():
+        note.wait_send()
+
     act(copies, "wait_send")
     act(vcopies, "wait_send")
 
@@ -515,13 +570,16 @@
             pltpu.SMEM((1, 6), jnp.int32),
             pltpu.VMEM((1, COMPONENTS, SLAB, CELL * CELL), BF16),
             pltpu.VMEM((3, PATCH_ROWS, TILE), BF16),
-            pltpu.VMEM((3 * TERMS, TILE, TILE), BF16),
-            pltpu.VMEM((3 * TERMS, TILE, TILE), BF16),
-            pltpu.VMEM((3, HALO, 128), BF16),
+            pltpu.VMEM((4 * TERMS, TILE, TILE), BF16),
+            pltpu.VMEM((4 * TERMS, TILE, TILE), BF16),
+            pltpu.VMEM((4, HALO, 128), BF16),
             pltpu.VMEM((12, 128, TILE), BF16),
-            pltpu.VMEM((12, HALO, TILE), F32),
-            pltpu.VMEM((3, 12, 8, 128), F32),
+            pltpu.VMEM((3, 12, HALO, TILE), F32),
+            pltpu.VMEM((COMPONENTS, 128, 128), F32),
+            pltpu.VMEM((4, 12, 8, 128), F32),
+            pltpu.VMEM((1, 12, 8, 128), F32),
             pltpu.VMEM((3, 11, 8, 128), F32),
+            pltpu.VMEM((2, 8, TILE), jnp.int32),
             pltpu.SemaphoreType.DMA((5,)),
             pltpu.SemaphoreType.DMA((3, PIECES)),
             pltpu.SemaphoreType.DMA((MEMBERS, PIECES)),
@@ -531,6 +589,8 @@
             pltpu.SemaphoreType.DMA((2,)),
             pltpu.SemaphoreType.DMA((2,)),
             pltpu.SemaphoreType.DMA((2,)),
+            pltpu.SemaphoreType.DMA((1,)),
+            pltpu.SemaphoreType.DMA((1,)),
         ],
         compiler_params=pltpu.CompilerParams(
             collective_id=0, has_side_effects=True, vmem_limit_bytes=40 << 20

time: 30.9 us -> 29.1 us (0.942)
  Pallas kernels: 27.9 us -> 26.1 us
    pallas_call x1, Pallas kernels: 27.9 us -> 26.1 us  [body(): pl.pallas_call(functools.partial(kernel, patches), out_shape=out, in_spec...]
where the time goes in v4:
time: 29.1 us; the launch traced here: 28.9 us
  Pallas kernels  26.1 us (90%)
  local copies, waits for them, and re-layouts  1.49 us (5%)
  between operations  1.36 us (5%)
    pallas_call x1, Pallas kernels, body(): pl.pallas_call(functools.partial(kernel, patches), out_shape=out, in_spec...  26.1 us
    unnamed x8, local copies, waits for them, and re-layouts  0.8 us
    slice x1, local copies, waits for them, and re-layouts, body(): return (both[:, :3], both[:, 3:])  0.69 us

profile of v4, /device:TPU:32, one launch (start us, length us, event | category | flops | bytes accessed | tf_op | source)
XLA Modules:
  0.0 28.9 jit_solution(2290054228041214789)
XLA Ops:
  0.6 0.0 copy-start.3
  0.6 0.0 copy-start.2
  0.7 0.0 copy-start.1
  1.3 0.0 copy-done.3
  1.3 0.0 copy-done.2
  1.4 0.0 copy-done.1
  1.4 0.0 copy-start
  1.4 0.8 %copy-done = bf16[1,3,8,1024]{3,2,1,0:T(8,128)(2,1)S(1)} copy-done((bf16[1,3,8,1024]{3,2,1,0:T(8,128)(2,1)S(1)}, bf16[1,3,8,1024]{3,2,1,0:T(8,128)(2,1)}, u32[]{:S(2)}) %copy-start) | copy-done | bytes 49176
  2.2 26.1 %shard_map.68 = f32[1,6,8,1024]{3,2,1,0:T(8,128)S(1)} custom-call(s32[1,3]{1,0:T(1,128)S(1)} %copy-done.1, s32[1,3]{1,0:T(1,128)S(1)} %copy-done.2, s32[1]{0:T(128)S(6)} %copy.7.cnt_hbm, s32[1,6]{1,0:T(1,128)S(1)} %copy-done.3, bf16[1,3,8,1024]{3,2,1,0:T(8,128)(2,1)S(1)} %copy-done), custom_call_target="tpu_custom_call" | custom-call | tf_op jit(solution)/shard_map/pallas_call | solution.py:561
  28.2 0.7 %fusion = (f32[1,3,8,1024]{3,2,1,0:T(8,128)}, f32[1,3,8,1024]{3,2,1,0:T(8,128)}) fusion(f32[1,6,8,1024]{3,2,1,0:T(8,128)S(1)} %shard_map.68), kind=kLoop, calls=%fused_computation | loop fusion | bytes 393216 | tf_op jit(solution)/shard_map/slice | solution.py:599
Async XLA Ops:
  0.6 0.7 %copy-start.3 = (s32[1,6]{1,0:T(1,128)S(1)}, s32[1,6]{1,0:T(1,128)}, u32[]{:S(2)}) copy-start(s32[1,6]{1,0:T(1,128)} %nb_hbm.1) | copy-start | bytes 76
  0.6 0.7 %copy-start.2 = (s32[1,3]{1,0:T(1,128)S(1)}, s32[1,3]{1,0:T(1,128)}, u32[]{:S(2)}) copy-start(s32[1,3]{1,0:T(1,128)} %off_hbm.1) | copy-start | bytes 40
  0.7 0.7 %copy-start.1 = (s32[1,3]{1,0:T(1,128)S(1)}, s32[1,3]{1,0:T(1,128)}, u32[]{:S(2)}) copy-start(s32[1,3]{1,0:T(1,128)} %src_hbm.1) | copy-start | bytes 40
  1.4 0.8 %copy-start = (bf16[1,3,8,1024]{3,2,1,0:T(8,128)(2,1)S(1)}, bf16[1,3,8,1024]{3,2,1,0:T(8,128)(2,1)}, u32[]{:S(2)}) copy-start(bf16[1,3,8,1024]{3,2,1,0:T(8,128)(2,1)} %vort_hbm.1) | copy-start | bytes 147460

commit v5 on v4

--- a/solution.py
+++ b/solution.py
@@ -99,7 +99,7 @@
     lx_ref[position] = (table * weight * live).astype(BF16)
 
 
-def zy_products(position, part, gbuf, wz_ref, wy_ref, rbuf):
+def zy_products(position, part, gbuf, wz_ref, wy_ref, sbuf, rbuf):
     slots = MEMBERS // PARTS[position]
     rows = slots * CHUNK
     lower = iota((slots, 24, 128), 2) < 64
@@ -121,8 +121,11 @@
             joined = jnp.concatenate(block, axis=2)
             for i in range(COMPONENTS):
                 pieces.append(joined[:, 8 * i : 8 * i + 8].reshape(8 * slots, TILE))
-        swapped = jnp.concatenate(pieces, axis=0).astype(BF16)
-        along_y = jnp.dot(swapped, wy_ref[position * TERMS + k], preferred_element_type=F32).astype(BF16)
+        sbuf[k, :rows] = jnp.concatenate(pieces, axis=0).astype(BF16)
+    for k in range(TERMS):
+        along_y = jnp.dot(
+            sbuf[k, :rows], wy_ref[position * TERMS + k], preferred_element_type=F32
+        ).astype(BF16)
         at = (part * TERMS + k) * 8 * slots
         rbuf[:, at : at + 8 * slots, :] = along_y.reshape(12, 8 * slots, TILE)
 
@@ -266,7 +269,7 @@
 
 def kernel(patches, src_hbm, off_hbm, cnt_hbm, nb_hbm, vort_hbm, out_ref,
            src_ref, off_ref, cnt_ref, nb_ref, vort_ref,
-           gbuf, wz_ref, wy_ref, lx_ref, rbuf, acc, potential, pbuf, back, vbuf, info,
+           gbuf, wz_ref, wy_ref, lx_ref, sbuf, rbuf, acc, potential, pbuf, back, vbuf, info,
            isem, xsend, msend, csend, grecv, psend, precv, vsend, vrecv, nsend, nrecv):
     patch = lax.axis_index("patch")
     member = lax.axis_index("comp")
@@ -361,7 +364,7 @@
             for step in STEPS[part * rows : part * rows + rows]:
                 for piece in pieces if step in waiting else ():
                     arrived(position, step, piece)
-            zy_products(position, part, gbuf, wz_ref, wy_ref, rbuf)
+            zy_products(position, part, gbuf, wz_ref, wy_ref, sbuf, rbuf)
         x_products(position, total, lx_ref, rbuf, acc, first)
 
     note = pltpu.make_async_remote_copy(
@@ -378,7 +381,8 @@
         )
         note.start()
 
-    tables(OWN)
+    for position in (OWN, MATE, FAR):
+        tables(position)
     for piece in pieces:
         for step in (1, 3):
             arrived(0, step, piece)
@@ -395,12 +399,11 @@
             arrived(2, 0, piece)
             opposite(piece).start()
 
-    zy_products(OWN, 0, gbuf, wz_ref, wy_ref, rbuf)
+    zy_products(OWN, 0, gbuf, wz_ref, wy_ref, sbuf, rbuf)
     for piece in pieces:
         arrived(0, 2, piece)
         to_mate(2, piece).start()
-    tables(MATE)
-    zy_products(OWN, 1, gbuf, wz_ref, wy_ref, rbuf)
+    zy_products(OWN, 1, gbuf, wz_ref, wy_ref, sbuf, rbuf)
     x_products(OWN, 0, lx_ref, rbuf, acc, True)
     products(MATE, STEPS, 0, False)
 
@@ -471,7 +474,22 @@
     def _():
         pack_potential(near, into(pbuf, 3))
         copies[0].start()
-        tables(FAR)
+        products(FAR, STEPS[1:], 2, True)
+        far = potential_of(acc, 2)
+        for i in range(COMPONENTS):
+            potential[i] = potential[i] + far[i]
+
+    @pl.when(jnp.logical_not(inner))
+    def _():
+        pbuf[FAR] = jnp.zeros(pbuf.shape[1:], F32)
+        vbuf[FAR] = jnp.zeros(vbuf.shape[1:], F32)
+
+    px, py, pz = [potential[i] for i in range(COMPONENTS)]
+    pack_potential((px, py, pz), into(pbuf, 0))
+    copies[1].start()
+
+    @pl.when(inner)
+    def _():
         note.wait_recv()
         sent = info[1]
         write_tables(
@@ -480,22 +498,6 @@
         )
         products(BACK, (), 1, True)
         pack_potential(potential_of(acc, 1), into(back, 0))
-        products(FAR, STEPS[1:], 2, True)
-        far = potential_of(acc, 2)
-        for i in range(COMPONENTS):
-            potential[i] = potential[i] + far[i]
-
-    @pl.when(jnp.logical_not(inner))
-    def _():
-        pbuf[FAR] = jnp.zeros(pbuf.shape[1:], F32)
-        vbuf[FAR] = jnp.zeros(vbuf.shape[1:], F32)
-
-    px, py, pz = [potential[i] for i in range(COMPONENTS)]
-    pack_potential((px, py, pz), into(pbuf, 0))
-    copies[1].start()
-
-    @pl.when(inner)
-    def _():
         copies[0].wait_recv()
         pbuf[FAR] = pbuf[FAR] + back[0]
 
@@ -573,6 +575,7 @@
             pltpu.VMEM((4 * TERMS, TILE, TILE), BF16),
             pltpu.VMEM((4 * TERMS, TILE, TILE), BF16),
             pltpu.VMEM((4, HALO, 128), BF16),
+            pltpu.VMEM((TERMS, PATCH_ROWS, TILE), BF16),
             pltpu.VMEM((12, 128, TILE), BF16),
             pltpu.VMEM((3, 12, HALO, TILE), F32),
             pltpu.VMEM((COMPONENTS, 128, 128), F32),

time: 29.1 us -> 28.9 us (level)
  Pallas kernels: 26.1 us -> 25.8 us
where the time goes in v5:
time: 28.9 us; the launch traced here: 28.7 us
  Pallas kernels  25.8 us (89%)
  local copies, waits for them, and re-layouts  1.49 us (5%)
  between operations  1.36 us (5%)
    pallas_call x1, Pallas kernels, body(): pl.pallas_call(functools.partial(kernel, patches), out_shape=out, in_spec...  25.8 us
    unnamed x8, local copies, waits for them, and re-layouts  0.8 us
    slice x1, local copies, waits for them, and re-layouts, body(): return (both[:, :3], both[:, 3:])  0.69 us

profile of v5, /device:TPU:32, one launch (start us, length us, event | category | flops | bytes accessed | tf_op | source)
XLA Modules:
  0.0 28.7 jit_solution(18036812302997449368)
XLA Ops:
  0.6 0.0 copy-start.3
  0.6 0.0 copy-start.2
  0.7 0.0 copy-start.1
  1.3 0.0 copy-done.3
  1.3 0.0 copy-done.2
  1.4 0.0 copy-done.1
  1.4 0.0 copy-start
  1.4 0.8 %copy-done = bf16[1,3,8,1024]{3,2,1,0:T(8,128)(2,1)S(1)} copy-done((bf16[1,3,8,1024]{3,2,1,0:T(8,128)(2,1)S(1)}, bf16[1,3,8,1024]{3,2,1,0:T(8,128)(2,1)}, u32[]{:S(2)}) %copy-start) | copy-done | bytes 49176
  2.2 25.8 %shard_map.68 = f32[1,6,8,1024]{3,2,1,0:T(8,128)S(1)} custom-call(s32[1,3]{1,0:T(1,128)S(1)} %copy-done.1, s32[1,3]{1,0:T(1,128)S(1)} %copy-done.2, s32[1]{0:T(128)S(6)} %copy.7.cnt_hbm, s32[1,6]{1,0:T(1,128)S(1)} %copy-done.3, bf16[1,3,8,1024]{3,2,1,0:T(8,128)(2,1)S(1)} %copy-done), custom_call_target="tpu_custom_call" | custom-call | tf_op jit(solution)/shard_map/pallas_call | solution.py:563
  28.0 0.7 %fusion = (f32[1,3,8,1024]{3,2,1,0:T(8,128)}, f32[1,3,8,1024]{3,2,1,0:T(8,128)}) fusion(f32[1,6,8,1024]{3,2,1,0:T(8,128)S(1)} %shard_map.68), kind=kLoop, calls=%fused_computation | loop fusion | bytes 393216 | tf_op jit(solution)/shard_map/slice | solution.py:602
Async XLA Ops:
  0.6 0.7 %copy-start.3 = (s32[1,6]{1,0:T(1,128)S(1)}, s32[1,6]{1,0:T(1,128)}, u32[]{:S(2)}) copy-start(s32[1,6]{1,0:T(1,128)} %nb_hbm.1) | copy-start | bytes 76
  0.6 0.7 %copy-start.2 = (s32[1,3]{1,0:T(1,128)S(1)}, s32[1,3]{1,0:T(1,128)}, u32[]{:S(2)}) copy-start(s32[1,3]{1,0:T(1,128)} %off_hbm.1) | copy-start | bytes 40
  0.7 0.7 %copy-start.1 = (s32[1,3]{1,0:T(1,128)S(1)}, s32[1,3]{1,0:T(1,128)}, u32[]{:S(2)}) copy-start(s32[1,3]{1,0:T(1,128)} %src_hbm.1) | copy-start | bytes 40
  1.4 0.8 %copy-start = (bf16[1,3,8,1024]{3,2,1,0:T(8,128)(2,1)S(1)}, bf16[1,3,8,1024]{3,2,1,0:T(8,128)(2,1)}, u32[]{:S(2)}) copy-start(bf16[1,3,8,1024]{3,2,1,0:T(8,128)(2,1)} %vort_hbm.1) | copy-start | bytes 147460

commit v6 on v5

--- a/solution.py
+++ b/solution.py
@@ -190,11 +190,16 @@
     )
 
 
-def grad_z(field, above, below):
+def grad_z(field):
     z = iota(field.shape, 1) & 31
-    higher = jnp.where(z == 31, above, lane_roll(field, -1))
-    lower = jnp.where(z == 0, below, lane_roll(field, 1))
+    higher = jnp.where(z == 31, 0.0, lane_roll(field, -1))
+    lower = jnp.where(z == 0, 0.0, lane_roll(field, 1))
     return 0.5 * (higher - lower)
+
+
+def ghost_z(above, below):
+    z = iota(above.shape, 1) & 31
+    return 0.5 * (jnp.where(z == 31, above, 0.0) - jnp.where(z == 0, below, 0.0))
 
 
 def pack_y(field, rows):
@@ -202,15 +207,21 @@
     return jnp.where(lower, field[:rows], field[7 * rows :])
 
 
-def grad_y(field, ghost, rows):
+def grad_y(field, rows):
     lane = iota(field.shape, 1)
+    none = jnp.zeros((rows, 128), F32)
     moved = lane_roll(field, -32)
-    following = jnp.concatenate([moved[rows:], lane_roll(ghost, -32)], axis=0)
-    higher = jnp.where(lane < 96, moved, following)
+    higher = jnp.where(lane < 96, moved, jnp.concatenate([moved[rows:], none], axis=0))
     moved = lane_roll(field, 32)
-    previous = jnp.concatenate([lane_roll(ghost, 32), moved[:-rows]], axis=0)
-    lower = jnp.where(lane >= 32, moved, previous)
+    lower = jnp.where(lane >= 32, moved, jnp.concatenate([none, moved[:-rows]], axis=0))
     return 0.5 * (higher - lower)
+
+
+def ghost_y(ghost, rows):
+    lane = iota((rows, 128), 1)
+    top = 0.5 * jnp.where(lane < 96, 0.0, lane_roll(ghost, -32))
+    bottom = -0.5 * jnp.where(lane >= 32, 0.0, lane_roll(ghost, 32))
+    return jnp.concatenate([bottom, jnp.zeros((6 * rows, 128), F32), top], axis=0)
 
 
 def halves(field):
@@ -241,35 +252,49 @@
     return above, below
 
 
-def grad_x(field, packed, member, own_only):
+def grad_x(field, member, own_only):
     low, high = halves(field)
-    above, below = unpack_x(packed)
     row = iota(low.shape, 1)
     device = jnp.full(low.shape, member, jnp.int32)
     first = device == 0
     last = device == MEMBERS - 1
     moved_low = pltpu.roll(low, 7, 1)
     moved_high = pltpu.roll(high, 7, 1)
-    up_low = jnp.where(row == 7, jnp.where(last, above, moved_high), moved_low)
+    up_low = jnp.where(row == 7, jnp.where(last, 0.0, moved_high), moved_low)
     back_low = pltpu.roll(low, 1, 1)
     back_high = pltpu.roll(high, 1, 1)
-    down_low = jnp.where(row == 0, jnp.where(first, below, back_high), back_low)
+    down_low = jnp.where(row == 0, jnp.where(first, 0.0, back_high), back_low)
     own = 0.5 * (up_low - down_low)
     if own_only:
         return own.reshape(64, 128)
-    up_high = jnp.where(row == 7, jnp.where(first, above, moved_low), moved_high)
-    down_high = jnp.where(row == 0, jnp.where(last, below, back_low), back_high)
+    up_high = jnp.where(row == 7, jnp.where(first, 0.0, moved_low), moved_high)
+    down_high = jnp.where(row == 0, jnp.where(last, 0.0, back_low), back_high)
     other = 0.5 * (up_high - down_high)
     return jnp.stack([own, other], axis=1).reshape(128, 128)
 
 
+def ghost_x(packed, member, own_only):
+    above, below = unpack_x(packed)
+    row = iota(above.shape, 1)
+    device = jnp.full(above.shape, member, jnp.int32)
+    first = device == 0
+    last = device == MEMBERS - 1
+    above = 0.5 * jnp.where(row == 7, above, 0.0)
+    below = 0.5 * jnp.where(row == 0, below, 0.0)
+    own = jnp.where(last, above, 0.0) - jnp.where(first, below, 0.0)
+    if own_only:
+        return own.reshape(64, 128)
+    other = jnp.where(first, above, 0.0) - jnp.where(last, below, 0.0)
+    return jnp.stack([own, other], axis=1).reshape(128, 128)
+
+
 def own_rows(field):
     return halves(field)[0].reshape(64, 128)
 
 
 def kernel(patches, src_hbm, off_hbm, cnt_hbm, nb_hbm, vort_hbm, out_ref,
            src_ref, off_ref, cnt_ref, nb_ref, vort_ref,
-           gbuf, wz_ref, wy_ref, lx_ref, sbuf, rbuf, acc, potential, pbuf, back, vbuf, info,
+           gbuf, wz_ref, wy_ref, lx_ref, sbuf, rbuf, acc, potential, flow, turning, pbuf, back, vbuf, info,
            isem, xsend, msend, csend, grecv, psend, precv, vsend, vrecv, nsend, nrecv):
     patch = lax.axis_index("patch")
     member = lax.axis_index("comp")
@@ -487,6 +512,9 @@
     px, py, pz = [potential[i] for i in range(COMPONENTS)]
     pack_potential((px, py, pz), into(pbuf, 0))
     copies[1].start()
+    flow[0] = grad_y(pz, HALO) - grad_z(py)
+    flow[1] = grad_z(px) - grad_x(pz, member, False)
+    flow[2] = grad_x(py, member, False) - grad_y(px, HALO)
 
     @pl.when(inner)
     def _():
@@ -504,10 +532,11 @@
     copies[1].wait_recv()
     zs, ys, xs = ghosts(pbuf, HALO, 2, 2, 2)
     above, below = unpack_z(zs, 2, HALO)
-    vx = grad_y(pz, ys[1], HALO) - grad_z(py, above[1], below[1])
-    vy = grad_z(px, above[0], below[0]) - grad_x(pz, xs[1], member, False)
-    vz = grad_x(py, xs[0], member, False) - grad_y(px, ys[0], HALO)
-    velocity = [vx, vy, vz]
+    velocity = [
+        flow[0] + (ghost_y(ys[1], HALO) - ghost_z(above[1], below[1])),
+        flow[1] + (ghost_z(above[0], below[0]) - ghost_x(xs[1], member, False)),
+        flow[2] + (ghost_x(xs[0], member, False) - ghost_y(ys[0], HALO)),
+    ]
     own = [own_rows(v) for v in velocity]
     packs = pack_z(own, 8) + [pack_y(v, 8) for v in own]
     for index, part in enumerate(packs):
@@ -519,18 +548,25 @@
     for i in range(COMPONENTS):
         for v in range(8):
             out_ref[0, i, :, 128 * v : 128 * v + 128] = own[i][8 * v : 8 * v + 8]
-    act(vcopies, "wait_recv")
-    zs, ys, xs = ghosts(vbuf, 8, 3, 3, 3)
-    above, below = unpack_z(zs, 3, 8)
     spin = [
         jnp.concatenate([vort_ref[0, i, :, 128 * v : 128 * v + 128].astype(F32) for v in range(8)], axis=0)
         for i in range(COMPONENTS)
     ]
     for i in range(COMPONENTS):
-        total = (
-            spin[0] * grad_x(velocity[i], xs[i], member, True)
-            + spin[1] * grad_y(own[i], ys[i], 8)
-            + spin[2] * grad_z(own[i], above[i], below[i])
+        flow[i, :64] = (
+            spin[0] * grad_x(velocity[i], member, True)
+            + spin[1] * grad_y(own[i], 8)
+            + spin[2] * grad_z(own[i])
+        )
+        turning[i] = spin[i]
+    act(vcopies, "wait_recv")
+    zs, ys, xs = ghosts(vbuf, 8, 3, 3, 3)
+    above, below = unpack_z(zs, 3, 8)
+    for i in range(COMPONENTS):
+        total = flow[i, :64] + (
+            turning[0] * ghost_x(xs[i], member, True)
+            + turning[1] * ghost_y(ys[i], 8)
+            + turning[2] * ghost_z(above[i], below[i])
         )
         for v in range(8):
             out_ref[0, 3 + i, :, 128 * v : 128 * v + 128] = total[8 * v : 8 * v + 8]
@@ -579,6 +615,8 @@
             pltpu.VMEM((12, 128, TILE), BF16),
             pltpu.VMEM((3, 12, HALO, TILE), F32),
             pltpu.VMEM((COMPONENTS, 128, 128), F32),
+            pltpu.VMEM((COMPONENTS, 128, 128), F32),
+            pltpu.VMEM((COMPONENTS, 64, 128), F32),
             pltpu.VMEM((4, 12, 8, 128), F32),
             pltpu.VMEM((1, 12, 8, 128), F32),
             pltpu.VMEM((3, 11, 8, 128), F32),

time: 28.9 us -> 28.7 us (level)
  no operation moved by 1% of the time
where the time goes in v6:
time: 28.7 us; the launch traced here: 28.5 us
  Pallas kernels  25.7 us (90%)
  local copies, waits for them, and re-layouts  1.49 us (5%)
  between operations  1.36 us (5%)
    pallas_call x1, Pallas kernels, body(): pl.pallas_call(functools.partial(kernel, patches), out_shape=out, in_spec...  25.7 us
    unnamed x8, local copies, waits for them, and re-layouts  0.8 us
    slice x1, local copies, waits for them, and re-layouts, body(): return (both[:, :3], both[:, 3:])  0.69 us

profile of v6, /device:TPU:32, one launch (start us, length us, event | category | flops | bytes accessed | tf_op | source)
XLA Modules:
  0.0 28.5 jit_solution(12270700887485285529)
XLA Ops:
  0.6 0.0 copy-start.3
  0.6 0.0 copy-start.2
  0.7 0.0 copy-start.1
  1.3 0.0 copy-done.3
  1.3 0.0 copy-done.2
  1.4 0.0 copy-done.1
  1.4 0.0 copy-start
  1.4 0.8 %copy-done = bf16[1,3,8,1024]{3,2,1,0:T(8,128)(2,1)S(1)} copy-done((bf16[1,3,8,1024]{3,2,1,0:T(8,128)(2,1)S(1)}, bf16[1,3,8,1024]{3,2,1,0:T(8,128)(2,1)}, u32[]{:S(2)}) %copy-start) | copy-done | bytes 49176
  2.2 25.7 %shard_map.68 = f32[1,6,8,1024]{3,2,1,0:T(8,128)S(1)} custom-call(s32[1,3]{1,0:T(1,128)S(1)} %copy-done.1, s32[1,3]{1,0:T(1,128)S(1)} %copy-done.2, s32[1]{0:T(128)S(6)} %copy.7.cnt_hbm, s32[1,6]{1,0:T(1,128)S(1)} %copy-done.3, bf16[1,3,8,1024]{3,2,1,0:T(8,128)(2,1)S(1)} %copy-done), custom_call_target="tpu_custom_call" | custom-call | tf_op jit(solution)/shard_map/pallas_call | solution.py:599
  27.8 0.7 %fusion = (f32[1,3,8,1024]{3,2,1,0:T(8,128)}, f32[1,3,8,1024]{3,2,1,0:T(8,128)}) fusion(f32[1,6,8,1024]{3,2,1,0:T(8,128)S(1)} %shard_map.68), kind=kLoop, calls=%fused_computation | loop fusion | bytes 393216 | tf_op jit(solution)/shard_map/slice | solution.py:640
Async XLA Ops:
  0.6 0.7 %copy-start.3 = (s32[1,6]{1,0:T(1,128)S(1)}, s32[1,6]{1,0:T(1,128)}, u32[]{:S(2)}) copy-start(s32[1,6]{1,0:T(1,128)} %nb_hbm.1) | copy-start | bytes 76
  0.6 0.7 %copy-start.2 = (s32[1,3]{1,0:T(1,128)S(1)}, s32[1,3]{1,0:T(1,128)}, u32[]{:S(2)}) copy-start(s32[1,3]{1,0:T(1,128)} %off_hbm.1) | copy-start | bytes 40
  0.7 0.7 %copy-start.1 = (s32[1,3]{1,0:T(1,128)S(1)}, s32[1,3]{1,0:T(1,128)}, u32[]{:S(2)}) copy-start(s32[1,3]{1,0:T(1,128)} %src_hbm.1) | copy-start | bytes 40
  1.4 0.8 %copy-start = (bf16[1,3,8,1024]{3,2,1,0:T(8,128)(2,1)S(1)}, bf16[1,3,8,1024]{3,2,1,0:T(8,128)(2,1)}, u32[]{:S(2)}) copy-start(bf16[1,3,8,1024]{3,2,1,0:T(8,128)(2,1)} %vort_hbm.1) | copy-start | bytes 147460

commit v7 on v6

--- a/solution.py
+++ b/solution.py
@@ -26,7 +26,7 @@
 PIECES = 1
 OWN, MATE, FAR, BACK = range(4)
 SOURCES = (OWN, MATE, FAR, OWN)
-PARTS = (2, 1, 2, 1)
+PARTS = (2, 2, 2, 1)
 
 
 def iota(shape, dim):
@@ -389,8 +389,8 @@
             for step in STEPS[part * rows : part * rows + rows]:
                 for piece in pieces if step in waiting else ():
                     arrived(position, step, piece)
-            zy_products(position, part, gbuf, wz_ref, wy_ref, sbuf, rbuf)
-        x_products(position, total, lx_ref, rbuf, acc, first)
+            zy_products(position, part, gbuf, wz_ref, wy_ref, sbuf, rbuf.at[OWN])
+        x_products(position, total, lx_ref, rbuf.at[OWN], acc, first)
 
     note = pltpu.make_async_remote_copy(
         src_ref=info.at[0], dst_ref=info.at[1], send_sem=nsend.at[0], recv_sem=nrecv.at[0],
@@ -424,13 +424,21 @@
             arrived(2, 0, piece)
             opposite(piece).start()
 
-    zy_products(OWN, 0, gbuf, wz_ref, wy_ref, sbuf, rbuf)
+    zy_products(OWN, 0, gbuf, wz_ref, wy_ref, sbuf, rbuf.at[OWN])
+    for step in (0, 1):
+        for piece in pieces:
+            arrived(MATE, step, piece)
+    zy_products(MATE, 0, gbuf, wz_ref, wy_ref, sbuf, rbuf.at[MATE])
     for piece in pieces:
-        arrived(0, 2, piece)
+        arrived(OWN, 2, piece)
         to_mate(2, piece).start()
-    zy_products(OWN, 1, gbuf, wz_ref, wy_ref, sbuf, rbuf)
-    x_products(OWN, 0, lx_ref, rbuf, acc, True)
-    products(MATE, STEPS, 0, False)
+    zy_products(OWN, 1, gbuf, wz_ref, wy_ref, sbuf, rbuf.at[OWN])
+    x_products(OWN, 0, lx_ref, rbuf.at[OWN], acc, True)
+    for step in (3, 2):
+        for piece in pieces:
+            arrived(MATE, step, piece)
+    zy_products(MATE, 1, gbuf, wz_ref, wy_ref, sbuf, rbuf.at[MATE])
+    x_products(MATE, 0, lx_ref, rbuf.at[MATE], acc, False)
 
     def exchange(buffer, places_from, send, recv):
         return [
@@ -612,7 +620,7 @@
             pltpu.VMEM((4 * TERMS, TILE, TILE), BF16),
             pltpu.VMEM((4, HALO, 128), BF16),
             pltpu.VMEM((TERMS, PATCH_ROWS, TILE), BF16),
-            pltpu.VMEM((12, 128, TILE), BF16),
+            pltpu.VMEM((2, 12, 128, TILE), BF16),
             pltpu.VMEM((3, 12, HALO, TILE), F32),
             pltpu.VMEM((COMPONENTS, 128, 128), F32),
             pltpu.VMEM((COMPONENTS, 128, 128), F32),

time: 28.7 us -> 28.8 us (level)
  no operation moved by 1% of the time
where the time goes in v7:
time: 28.8 us; the launch traced here: 28.6 us
  Pallas kernels  25.8 us (90%)
  local copies, waits for them, and re-layouts  1.49 us (5%)
  between operations  1.36 us (5%)
    pallas_call x1, Pallas kernels, body(): pl.pallas_call(functools.partial(kernel, patches), out_shape=out, in_spec...  25.8 us
    unnamed x8, local copies, waits for them, and re-layouts  0.8 us
    slice x1, local copies, waits for them, and re-layouts, body(): return (both[:, :3], both[:, 3:])  0.69 us

profile of v7, /device:TPU:32, one launch (start us, length us, event | category | flops | bytes accessed | tf_op | source)
XLA Modules:
  0.0 28.6 jit_solution(1053205834561509279)
XLA Ops:
  0.6 0.0 copy-start.3
  0.6 0.0 copy-start.2
  0.7 0.0 copy-start.1
  1.3 0.0 copy-done.3
  1.3 0.0 copy-done.2
  1.4 0.0 copy-done.1
  1.4 0.0 copy-start
  1.4 0.8 %copy-done = bf16[1,3,8,1024]{3,2,1,0:T(8,128)(2,1)S(1)} copy-done((bf16[1,3,8,1024]{3,2,1,0:T(8,128)(2,1)S(1)}, bf16[1,3,8,1024]{3,2,1,0:T(8,128)(2,1)}, u32[]{:S(2)}) %copy-start) | copy-done | bytes 49176
  2.2 25.8 %shard_map.68 = f32[1,6,8,1024]{3,2,1,0:T(8,128)S(1)} custom-call(s32[1,3]{1,0:T(1,128)S(1)} %copy-done.1, s32[1,3]{1,0:T(1,128)S(1)} %copy-done.2, s32[1]{0:T(128)S(6)} %copy.7.cnt_hbm, s32[1,6]{1,0:T(1,128)S(1)} %copy-done.3, bf16[1,3,8,1024]{3,2,1,0:T(8,128)(2,1)S(1)} %copy-done), custom_call_target="tpu_custom_call" | custom-call | tf_op jit(solution)/shard_map/pallas_call | solution.py:607
  28.0 0.7 %fusion = (f32[1,3,8,1024]{3,2,1,0:T(8,128)}, f32[1,3,8,1024]{3,2,1,0:T(8,128)}) fusion(f32[1,6,8,1024]{3,2,1,0:T(8,128)S(1)} %shard_map.68), kind=kLoop, calls=%fused_computation | loop fusion | bytes 393216 | tf_op jit(solution)/shard_map/slice | solution.py:648
Async XLA Ops:
  0.6 0.7 %copy-start.3 = (s32[1,6]{1,0:T(1,128)S(1)}, s32[1,6]{1,0:T(1,128)}, u32[]{:S(2)}) copy-start(s32[1,6]{1,0:T(1,128)} %nb_hbm.1) | copy-start | bytes 76
  0.6 0.7 %copy-start.2 = (s32[1,3]{1,0:T(1,128)S(1)}, s32[1,3]{1,0:T(1,128)}, u32[]{:S(2)}) copy-start(s32[1,3]{1,0:T(1,128)} %off_hbm.1) | copy-start | bytes 40
  0.7 0.7 %copy-start.1 = (s32[1,3]{1,0:T(1,128)S(1)}, s32[1,3]{1,0:T(1,128)}, u32[]{:S(2)}) copy-start(s32[1,3]{1,0:T(1,128)} %src_hbm.1) | copy-start | bytes 40
  1.4 0.8 %copy-start = (bf16[1,3,8,1024]{3,2,1,0:T(8,128)(2,1)S(1)}, bf16[1,3,8,1024]{3,2,1,0:T(8,128)(2,1)}, u32[]{:S(2)}) copy-start(bf16[1,3,8,1024]{3,2,1,0:T(8,128)(2,1)} %vort_hbm.1) | copy-start | bytes 147460
